TPU v7x, 512 devices: a whole 4x8x8 slice. The times are simulated.
512 devices in a mesh: pts: 128 (over y, z, core), grp: 4 (over x).
Axes of the slice: x: 4, y: 8, z: 8, core: 2. Of those that a mesh axis runs over, the one named last changes fastest.
Arguments:
- jacobian: bfloat16 [65536, 3, 3, 384], P(('pts', 'grp')), may hold values from -0.15625 to 0.15625
- owner: int32 [65536, 1], P(('pts', 'grp')), may hold values from 0 to 127; in each aligned block of 128 rows (0 to 127, 128 to 255, ...) at most 2 rows name the same one
- damping: float32 [128, 384], P('pts'), may hold values from 0.2 to 2
Outputs:
- reduced_diag: float32 [128, 384, 384], P('pts', None, 'grp')
- reduced_pair: float32 [128, 384, 384], P('pts', None, 'grp')
Inputs may be any that keep to these rules, and one draw needn't show every extreme that they name: `owner`: among the 128 landmarks of one device at most 2 name the same segment, and in every draw some segment is named by exactly 2 landmarks of some device.
All inputs are finite; a program needn't handle non-finite values.
Results may differ from a plain program's by a relative error of at most 0.0003.
Values may be sent and summed in bfloat16 or wider, within the bound.
No kernel may reach another device: no remote copies, remote signals or barrier semaphores. Data moves between devices by JAX's collectives and lax.ppermute only.
A program may use at most 64 MiB of HBM per device.

v0:
```python
import jax
import jax.numpy as jnp
from jax import lax
from jax.sharding import Mesh
from jax.sharding import PartitionSpec as P

PTS = ("pts_0", "pts_1", "pts_2")
PTS_GRP = ("pts_0", "pts_1", "pts_2", "grp")


def in_blocks(value, dim, devices):
    before, after = (value.shape[:dim], value.shape[dim + 1 :])
    return jnp.moveaxis(value.reshape(*before, devices, -1, *after), dim, 0)


def joined_along(pieces, dim):
    pieces = jnp.moveaxis(pieces, 0, dim)
    shape = pieces.shape
    return pieces.reshape(*shape[:dim], shape[dim] * shape[dim + 1], *shape[dim + 2 :])


def exchange_in_order(pieces, axes, turns):
    inside = pieces.shape[1:]
    whole = pieces.reshape(*(lax.axis_size(a) for a in axes), *inside)
    for k in turns:
        whole = lax.all_to_all(whole, axes[k], k, k, tiled=True)
    return whole.reshape(-1, *inside)


def core_and_chips(value, groups, turns, split_dim, concat_dim):
    devices = lax.axis_size(groups[0]) * lax.axis_size(groups[1])
    pieces = in_blocks(value, split_dim, devices)
    return joined_along(exchange_in_order(pieces, groups, turns), concat_dim)


def packed_total(arrays, axis):
    line, at, outs = (jnp.concatenate([a.reshape(-1) for a in arrays]), 0, [])
    so_far = lax.psum(line, axis)
    for a in arrays:
        outs.append(so_far[at : at + a.size].reshape(a.shape))
        at += a.size
    return tuple(outs)


def sent_together(arrays, axis, dim, along):
    widths = [a.shape[along] for a in arrays]
    both = jnp.concatenate(arrays, axis=along)
    whole = lax.psum_scatter(both, axis, scatter_dimension=dim, tiled=True)
    return tuple(jnp.split(whole, [sum(widths[:k]) for k in range(1, len(widths))], axis=along))


def shifted(value, axis, by):
    devices = lax.axis_size(axis)
    return lax.ppermute(value, axis, [(i, (i + by) % devices) for i in range(devices)])


def gram(left, right):
    return lax.dot_general(
        left, right, (((0,), (0,)), ((), ())), preferred_element_type=jnp.float32
    )


def exact_gram(left, right):
    return lax.dot_general(
        left,
        right,
        (((0,), (0,)), ((), ())),
        precision=lax.Precision.HIGHEST,
        preferred_element_type=jnp.float32,
    )


def local(jacobian, owner, damping):
    points = jacobian.shape[0]
    width = jacobian.shape[3]
    owners = lax.axis_size(PTS)
    groups = lax.axis_size("grp")
    capacity = max(2, 2 * points // owners)
    slots = owners * capacity
    segment = owner[:, 0]
    same = segment[:, None] == segment[None, :]
    before = jnp.arange(points)[None, :] < jnp.arange(points)[:, None]
    rank = jnp.sum((same & before).astype(jnp.int32), axis=1)
    slot_of = segment * capacity + rank
    match = slot_of[None, :] == jnp.arange(slots, dtype=jnp.int32)[:, None]
    source = jnp.sum(match.astype(jnp.int32) * jnp.arange(points, dtype=jnp.int32)[None, :], axis=1)
    filled = jnp.any(match, axis=1)
    outgoing = jnp.where(
        filled[:, None, None, None], jacobian[source], jnp.zeros((), jacobian.dtype)
    )
    received = core_and_chips(outgoing, (("pts_0", "pts_1"), "pts_2"), (1, 0), 0, 0)
    columns = width // groups
    col_start = lax.axis_index("grp") * columns
    first = received[:, 0].reshape(-1, width)
    middle = received[:, 1].reshape(-1, width)
    last = received[:, 2].reshape(-1, width)
    d_odd, b_low, b_high = packed_total(
        (gram(middle, middle), gram(middle, first), gram(middle, last)), "grp"
    )
    d_low, d_high, e_pair = sent_together(
        (gram(first, first), gram(last, last), gram(first, last)), "grp", 1, 0
    )
    system = d_odd + jnp.diag(damping[0])
    factor = jnp.linalg.cholesky(system)
    y_low = lax.linalg.triangular_solve(factor, b_low, left_side=True, lower=True)
    y_high = lax.linalg.triangular_solve(factor, b_high, left_side=True, lower=True)
    y_low_cols = lax.dynamic_slice_in_dim(y_low, col_start, columns, 1)
    y_high_cols = lax.dynamic_slice_in_dim(y_high, col_start, columns, 1)
    low = d_low - exact_gram(y_low, y_low_cols)
    high = d_high - exact_gram(y_high, y_high_cols)
    pair = e_pair - exact_gram(y_low, y_high_cols)
    carried = shifted(high, PTS, 1)
    return ((low + carried)[None], pair[None])


def solution(mesh):
    torus = Mesh(
        mesh.devices.reshape(8, 8, 2, mesh.shape["grp"]), ("pts_0", "pts_1", "pts_2", "grp")
    )
    placed = (P(PTS_GRP, None, None, None), P(PTS_GRP, None), P(PTS, None))
    return jax.shard_map(
        local,
        mesh=torus,
        in_specs=placed,
        out_specs=(P(PTS, None, "grp"), P(PTS, None, "grp")),
        check_vma=False,
    )
```

profile of v0, /device:TPU:32, one launch (start us, length us, event | category | flops | bytes accessed | tf_op | source)
XLA Modules:
  0.0 299.1 jit_solution(6131619147207161383)
XLA Ops:
  7.2 0.9 convert_reduce_fusion
  8.1 0.7 multiply_add_fusion
  9.1 6.1 %gather_fusion = bf16[256,3,3,384]{3,0,2,1:T(8,128)(2,1)S(1)} fusion(bf16[128,3,3,384]{3,0,2,1:T(8,128)(2,1)S(1)} %copy-done, s32[1024]{0:T(1024)S(1)} %pad_clamp_fusion), kind=kCustom, calls=%fused_computation | custom fusion | bytes 3539968 | tf_op jit(solution)/shard_map/gather | solution.py:89
  15.2 2.1 gather.9
  17.5 3.3 %broadcast_select_fusion = bf16[64,2,2,3,3,384]{5,2,0,4,3,1:T(2,128)(2,1)S(1)} fusion(pred[64,2,2]{2,0,1:T(8,128)(4,1)S(1)} %copy.66, bf16[64,2,2,3,3,384]{5,2,1,0,4,3:T(2,128)(2,1)} %gather.9), kind=kLoop, calls=%fused_computation.3 | loop fusion | flops 884736 | bytes 3539200 | tf_op jit(solution)/shard_map/jit(_where)/select_n | solution.py:88
  20.8 5.2 %all_to_all.10 = bf16[64,2,2,3,3,384]{5,2,0,4,3,1:T(2,128)(2,1)S(1)} all-to-all(bf16[64,2,2,3,3,384]{5,2,0,4,3,1:T(2,128)(2,1)S(1)} %broadcast_select_fusion), channel_id=1, replica_groups=mesh['pts_0'=8,'pts_1'=8,'pts_2'=2,'grp'=4] {'pts_2'}, dimensions={1} | all-to-all | bytes 3538944 | tf_op jit(solution)/shard_map/all_to_all | solution.py:26
  25.9 1.2 copy.68
  27.2 70.1 %all_to_all.11 = bf16[64,2,2,3,3,384]{5,2,1,4,3,0:T(2,128)(2,1)S(1)} all-to-all(bf16[64,2,2,3,3,384]{5,2,1,4,3,0:T(2,128)(2,1)S(1)} %copy.68), channel_id=1, replica_groups=mesh['pts_0'=8,'pts_1'=8,'pts_2'=2,'grp'=4] {'pts_0','pts_1'}, dimensions={0} | all-to-all | bytes 3538944 | tf_op jit(solution)/shard_map/all_to_all | solution.py:26
  97.3 1.4 copy.69
  98.7 2.1 reshape_reshape.4
  100.8 1.9 convolution_bitcast_fusion.2
  102.7 1.7 convolution_bitcast_fusion.1
  104.4 0.5 convolution_bitcast_fusion
  105.1 1.3 pad_maximum_fusion.1
  106.5 0.6 copy-done.6
  107.1 0.8 copy-done.3
  108.4 0.5 convolution_bitcast_fusion.5
  108.9 0.5 convolution_bitcast_fusion.3
  109.5 1.9 copy.95
  111.5 58.7 %all-reduce.3.cloned.1.call-done = f32[442368]{0:T(1024)} async-done(((f32[442368]{0:T(1024)}), f32[442368]{0:T(1024)}) %all-reduce.3.cloned.1.call-update) | async-done | bytes 1769488 | tf_op jit(solution)/shard_map/psum | solution.py:38
  170.1 1.5 fusion.40
  172.1 1.1 copy.78
  173.2 1.1 fusion.3
  174.3 11.7 %cholesky.76 = f32[128,128]{1,0:T(8,128)S(1)} custom-call(f32[128,128]{1,0:T(8,128)S(1)} %cholesky.189), custom_call_target="Cholesky" | custom-call | tf_op jit(solution)/shard_map/jit(cholesky)/cholesky | solution.py:104
  186.1 9.8 %custom-call.22 = f32[1,128,128]{1,2,0:T(8,128)S(1)} custom-call(f32[1,128,128]{2,1,0:T(8,128)S(1)} %get-tuple-element.71), custom_call_target="InvertDiagBlocksLowerTriangular" | custom-call | tf_op jit(solution)/shard_map/jit(cholesky)/cholesky | solution.py:104
  196.5 11.7 %cholesky.160 = f32[128,128]{1,0:T(8,128)S(1)} custom-call(f32[128,128]{1,0:T(8,128)S(1)} %cholesky.193), custom_call_target="Cholesky" | custom-call | tf_op jit(solution)/shard_map/jit(cholesky)/cholesky | solution.py:104
  208.5 9.9 %custom-call.23 = f32[1,128,128]{1,2,0:T(8,128)S(1)} custom-call(f32[1,128,128]{2,1,0:T(8,128)S(1)} %get-tuple-element.69), custom_call_target="InvertDiagBlocksLowerTriangular" | custom-call | tf_op jit(solution)/shard_map/jit(cholesky)/cholesky | solution.py:104
  218.8 1.2 convolution_subtract_fusion.8
  220.1 11.7 %cholesky.179 = f32[128,128]{1,0:T(8,128)S(1)} custom-call(f32[128,128]{1,0:T(8,128)S(1)} %convolution_subtract_fusion.8), custom_call_target="Cholesky" | custom-call | tf_op jit(solution)/shard_map/jit(cholesky)/cholesky | solution.py:104
  231.9 0.7 compare_reduce_fusion
  232.6 0.7 compare_reduce_fusion.1
  235.2 8.2 %while.4 = (s32[]{:T(128)}, f32[384,384]{0,1:T(8,128)S(1)}, s32[3,2]{0,1:T(2,128)S(1)}, f32[3,128,128]{2,1,0:T(8,128)}, s32[]{:T(128)}) while((s32[]{:T(128)}, f32[384,384]{0,1:T(8,128)S(1)}, s32[3,2]{0,1:T(2,128)S(1)}, f32[3,128,128]{2,1,0:T(8,128)}, s32[]{:T(128)}) %tuple.43), condition=%wide.while_cond, body=%wide.while_body.sunk | while | flops 2 | bytes 393829 | solution.py:105
  235.3 0.5 fusion.51
  235.9 1.4 dynamic-slice.9
  237.3 0.6 bitcast_dynamic-update-slice_fusion.2
  238.0 0.5 fusion.51
  238.6 1.4 dynamic-slice.9
  240.1 0.6 bitcast_dynamic-update-slice_fusion.2
  240.8 0.5 fusion.51
  241.3 1.4 dynamic-slice.9
  242.8 0.6 bitcast_dynamic-update-slice_fusion.2
  243.4 30.6 %custom-call.25 = f32[3,128,128]{1,2,0:T(8,128)S(1)} custom-call(f32[3,128,128]{2,1,0:T(8,128)} %get-tuple-element.17), custom_call_target="InvertDiagBlocksLowerTriangular" | custom-call | tf_op jit(solution)/shard_map/triangular_solve/custom-call.2 | solution.py:105
  274.0 1.0 slice.135
  279.1 1.6 convolution_subtract_fusion.5
  280.7 1.9 collective-permute-start
  282.7 1.3 fusion
  284.0 6.5 %collective-permute-done = f32[384,96]{0,1:T(8,128)S(1)} collective-permute-done((f32[384,96]{0,1:T(8,128)S(1)}, f32[384,96]{0,1:T(8,128)S(1)}, u32[]{:S(2)}, u32[]{:S(2)}) %collective-permute-start) | collective-permute-done | bytes 147488 | tf_op jit(solution)/shard_map/ppermute | solution.py:54
  290.5 1.3 fusion.2
  (71 shorter events, 7.7 us)
Async XLA Ops:
  7.2 1.9 copy-start
  7.2 162.9 %all-reduce.3.cloned.1.call-start = ((), (), s32[]{:S(2)}) async-start(), calls=%async_computation.3 | async-start | bytes 3538944 | tf_op jit(solution)/shard_map/psum | solution.py:38
  100.8 3.6 %copy-start.2 = (bf16[256,3,3,384]{3,0,2,1:T(8,128)(2,1)S(1)}, bf16[256,3,3,384]{3,0,2,1:T(8,128)(2,1)}, u32[]{:S(2)}) copy-start(bf16[256,3,3,384]{3,0,2,1:T(8,128)(2,1)} %reshape_reshape.4) | copy-start | bytes 5308420
  106.4 0.7 copy-start.6
  106.4 1.5 copy-start.3
  106.4 172.7 %reduce-scatter.4.cloned.1.call-start = ((), (), s32[]{:S(2)}) async-start(), calls=%async_computation.4 | async-start | bytes 2211840
  174.3 34.2 %copy-start.4 = (f32[384,384]{1,0:T(8,128)}, f32[384,384]{1,0:T(8,128)S(1)}, u32[]{:S(2)}) copy-start(f32[384,384]{1,0:T(8,128)S(1)} %fusion.3) | copy-start | bytes 1769476
  275.5 1.6 copy-start.1
  279.1 3.6 %copy-start.5 = (f32[96,1152]{1,0:T(8,128)S(1)}, f32[96,1152]{1,0:T(8,128)}, u32[]{:S(2)}) copy-start(f32[96,1152]{1,0:T(8,128)} %reduce-scatter.4.cloned.1.call-done) | copy-start | bytes 1327108
  280.7 9.8 %collective-permute-start = (f32[384,96]{0,1:T(8,128)S(1)}, f32[384,96]{0,1:T(8,128)S(1)}, u32[]{:S(2)}, u32[]{:S(2)}) collective-permute-start(f32[384,96]{0,1:T(8,128)S(1)} %convolution_subtract_fusion.5), channel_id=1, source_target_pairs={{0,4},{4,8},{8,12},{12,16},{16,20},{20,24},{24,28},{28,32},{32,36}... | collective-permute-start | bytes 442376 | tf_op jit(solution)/shard_map/ppermute | solution.py:54
Sparse Core Ops, SparseCore 0:
  106.6 63.5 all-reduce.2
  173.2 32.2 reduce-scatter.3
where the time goes:
time: 302 us; the launch traced here: 299 us
  other arithmetic  94.8 us (31%)
  blocking collectives  75.3 us (25%)
  waiting for transfers between devices  65.2 us (22%)
  local copies, waits for them, and re-layouts  29.2 us (10%)
  between operations  16.9 us (6%)
  matrix products  15.7 us (5%)
    all_to_all x2, blocking collectives, exchange_in_order(): whole = lax.all_to_all(whole, axes[k], k, k, tiled=True)  75.3 us
    psum x1, waiting for transfers between devices, packed_total(): so_far = lax.psum(line, axis)  58.7 us
    another operation x10, other arithmetic, local(): factor = jnp.linalg.cholesky(system)  56.3 us
    another operation x5, other arithmetic, local(): lax.linalg.triangular_solve(factor, b_low, left_side=True, lower=True)  30.6 us
    gather x2, local copies, waits for them, and re-layouts, local(): jacobian[source]  8.25 us
    another operation x16, local copies, waits for them, and re-layouts, local(): lax.linalg.triangular_solve(factor, b_low, left_side=True, lower=True)  8.16 us
    ppermute x1, waiting for transfers between devices, shifted(): lax.ppermute(value, axis, [(i, (i + by) % devices) for i in range(devices)])  6.47 us
  transfers between devices with their start and end apart: 3, of which 2 were waited for; matrix products, arithmetic and copies ran while one was open for 37% of the time, Pallas kernels for 0%

commit v1 on v0

v1 whole, which is shorter than its diff:
```python
import jax
import jax.numpy as jnp
from jax import lax
from jax.experimental import pallas as pl
from jax.experimental.pallas import tpu as pltpu
from jax.sharding import Mesh
from jax.sharding import PartitionSpec as P

PTS = ("pts_0", "pts_1", "pts_2")
PTS_GRP = ("pts_0", "pts_1", "pts_2", "grp")
F32 = jnp.float32
BF16 = jnp.bfloat16
HI = lax.Precision.HIGHEST
NN = ((1,), (0,))
NT = ((1,), (1,))
TN = ((0,), (0,))
TILE = 128
PARAMS = pltpu.CompilerParams(vmem_limit_bytes=40 * 2**20)


def mm(a, b, dims, prec=None):
    return lax.dot_general(a, b, (dims, ((), ())), precision=prec, preferred_element_type=F32)


def call(body, outs, *args, cost=None, scratch=()):
    return pl.pallas_call(
        body, out_shape=outs, scratch_shapes=scratch, compiler_params=PARAMS, cost_estimate=cost
    )(*args)


def cost(flops, nbytes):
    return pl.CostEstimate(flops=flops, bytes_accessed=nbytes, transcendentals=0)


def pack_body(capacity, owner_ref, rows_ref, out_ref):
    clusters, sets, points, width = rows_ref.shape
    slots = out_ref.shape[0] * capacity
    owner = owner_ref[...]
    slot = lax.broadcasted_iota(jnp.int32, (slots, points), 0)
    hit = jnp.where(owner == slot // capacity, 1.0, 0.0)
    upper = jnp.where(
        lax.broadcasted_iota(jnp.int32, (points, points), 0)
        < lax.broadcasted_iota(jnp.int32, (points, points), 1),
        1.0,
        0.0,
    )
    before = mm(hit.astype(BF16), upper.astype(BF16), NN)
    pick = jnp.where(before == (slot % capacity).astype(F32), hit, 0.0).astype(BF16)
    for k in range(clusters):
        for r in range(sets):
            at = (k * sets + r) * width
            rows = mm(pick, rows_ref[k, r], NN).astype(BF16)
            out_ref[:, :, at : at + width] = rows.reshape(-1, capacity, width)


def cluster_rows(ref, k):
    width = ref.shape[2] // 9
    at = k * 3 * width
    flat = ref[:, :, at : at + 3 * width].reshape(-1, 3 * width)
    return [flat[:, r * width : (r + 1) * width] for r in range(3)]


def summed_gram(left, right):
    return mm(left[0], right[0], TN) + mm(left[1], right[1], TN) + mm(left[2], right[2], TN)


def odd_body(rows_ref, out_ref):
    mid = cluster_rows(rows_ref, 1)
    full = summed_gram(mid, mid)
    at = 0
    for i in range(full.shape[0] // TILE):
        for j in range(i + 1):
            out_ref[at : at + TILE] = full[i * TILE : (i + 1) * TILE, j * TILE : (j + 1) * TILE]
            at += TILE


def side_body(rows_ref, out_ref):
    width = out_ref.shape[0]
    mid = cluster_rows(rows_ref, 1)
    out_ref[:, :width] = summed_gram(cluster_rows(rows_ref, 0), mid)
    out_ref[:, width:] = summed_gram(cluster_rows(rows_ref, 2), mid)


def even_body(rows_ref, out_ref):
    width = out_ref.shape[0]
    first, last = cluster_rows(rows_ref, 0), cluster_rows(rows_ref, 2)
    out_ref[:, :width] = summed_gram(first, first)
    out_ref[:, width : 2 * width] = summed_gram(last, last)
    out_ref[:, 2 * width :] = summed_gram(last, first)


def sum_body(parts_ref, out_ref):
    total = parts_ref[0]
    for k in range(1, parts_ref.shape[0]):
        total = total + parts_ref[k]
    for k in range(out_ref.shape[0]):
        out_ref[k] = total


def eye(n):
    rows = lax.broadcasted_iota(jnp.int32, (n, n), 0)
    return jnp.where(rows == lax.broadcasted_iota(jnp.int32, (n, n), 1), 1.0, 0.0).astype(F32)


def factor_tile(a_ref, w_ref, panel):
    n = a_ref.shape[0]
    row = lax.broadcasted_iota(jnp.int32, (panel, n), 0)
    for b in range(0, n, panel):
        pa = a_ref[b : b + panel, :]
        pw = w_ref[b : b + panel, :]
        cols = [jnp.broadcast_to(pa[:, b + k : b + k + 1], (panel, n)) for k in range(panel)]
        scale = jnp.ones((panel, n), F32)
        for j in range(panel):
            pivot = jnp.broadcast_to(cols[j][j : j + 1, :], (panel, n))
            scale = jnp.where(row == j, pivot, scale)
            m = jnp.where(row > j, cols[j] / pivot, 0.0)
            for k in range(j + 1, panel):
                cols[k] = cols[k] - m * cols[k][j : j + 1, :]
            pa = pa - m * pa[j : j + 1, :]
            pw = pw - m * pw[j : j + 1, :]
        rs = lax.rsqrt(scale)
        pa = pa * rs
        pw = pw * rs
        w_ref[b : b + panel, :] = pw
        if b + panel < n:
            u = mm(pa, jnp.concatenate([pa, pw], axis=1), TN, HI)
            a_ref[b + panel :, :] = a_ref[b + panel :, :] - u[b + panel :, :n]
            w_ref[b + panel :, :] = w_ref[b + panel :, :] - u[b + panel :, n:]


def factor_body(blocks_ref, damping_ref, out_ref, a_ref, w_ref):
    n = TILE
    count = damping_ref.shape[1] // n
    at, s = 0, []
    for i in range(count):
        s.append([])
        for j in range(i + 1):
            s[i].append(blocks_ref[at : at + n])
            at += n
    for i in range(count):
        s[i][i] = s[i][i] + eye(n) * damping_ref[:, i * n : (i + 1) * n]
    for d in range(count):
        a_ref[...] = s[d][d]
        w_ref[...] = eye(n)
        factor_tile(a_ref, w_ref, 32)
        w = w_ref[...]
        out_ref[(d * (d + 1) // 2 + d) * n : (d * (d + 1) // 2 + d + 1) * n] = w
        for i in range(d + 1, count):
            s[i][d] = mm(s[i][d], w, NT, HI)
            out_ref[(i * (i + 1) // 2 + d) * n : (i * (i + 1) // 2 + d + 1) * n] = s[i][d]
        for i in range(d + 1, count):
            for k in range(d + 1, i + 1):
                s[i][k] = s[i][k] - mm(s[i][d], s[k][d], NT, HI)


def solve_body(factor_ref, right_ref, low_ref, high_ref):
    n = TILE
    rows, width = right_ref.shape[1], right_ref.shape[2] // 2
    count = width // n
    block = lambda i, j: factor_ref[(i * (i + 1) // 2 + j) * n : (i * (i + 1) // 2 + j + 1) * n]
    right = right_ref[0]
    for k in range(1, right_ref.shape[0]):
        right = right + right_ref[k]
    right = jnp.concatenate([right[:, :width], right[:, width:]], axis=0)
    done = []
    for i in range(count):
        part = right[:, i * n : (i + 1) * n]
        for j in range(i):
            part = part - mm(done[j], block(i, j), NT, HI)
        done.append(mm(part, block(i, i), NT, HI))
        for k in range(low_ref.shape[0]):
            low_ref[k, :, i * n : (i + 1) * n] = done[i][:rows]
            high_ref[k, :, i * n : (i + 1) * n] = done[i][rows:]


def whole(ref):
    return jnp.concatenate([ref[k] for k in range(ref.shape[0])], axis=0)


def high_body(y_ref, mine_ref, even_ref, out_ref):
    width = y_ref.shape[2]
    out_ref[...] = even_ref[:, width : 2 * width] - mm(mine_ref[0], whole(y_ref), NT, HI)


def low_body(y_ref, low_mine_ref, high_mine_ref, even_ref, low_ref, pair_ref):
    width = y_ref.shape[2]
    y_low = whole(y_ref)
    low_ref[...] = even_ref[:, :width] - mm(low_mine_ref[0], y_low, NT, HI)
    pair_ref[...] = even_ref[:, 2 * width :] - mm(high_mine_ref[0], y_low, NT, HI)


def exchanged(value, axis):
    return lax.all_to_all(value, axis, 0, 0, tiled=True)


def after(value, other):
    return lax.optimization_barrier((value, other))[0]


def shape(*dims):
    return jax.ShapeDtypeStruct(dims, F32)


def local(jacobian, owner, damping):
    points, _, _, width = jacobian.shape
    owners = lax.axis_size(PTS)
    groups = lax.axis_size("grp")
    columns = width // groups
    capacity = max(2, 2 * points // owners)
    rows = jnp.transpose(jacobian, (1, 2, 0, 3))
    segment = owner.reshape(1, points)
    tiles = (width // TILE) * (width // TILE + 1) // 2

    sent = call(
        lambda *refs: pack_body(capacity, *refs),
        jax.ShapeDtypeStruct((owners, capacity, 9 * width), BF16),
        segment,
        rows,
    )
    got = exchanged(sent, PTS)
    odd = call(odd_body, shape(tiles * TILE, TILE), got, cost=cost(10**9, 10**6))
    odd = exchanged(odd.reshape(groups, -1, TILE), "grp")
    odd = call(sum_body, shape(*odd.shape), odd)
    odd = exchanged(odd, "grp").reshape(-1, TILE)
    even = call(even_body, shape(width, 3 * width), got, cost=cost(10**9, 10**6))
    even = lax.psum_scatter(even, "grp", scatter_dimension=0, tiled=True)
    side = call(side_body, shape(width, 2 * width), got, cost=cost(10**9, 10**6))
    side = after(side, odd)
    side = exchanged(side.reshape(groups, columns, 2 * width), "grp")
    factor = call(
        factor_body,
        shape(tiles * TILE, TILE),
        odd,
        damping,
        cost=cost(10**10, 10**6),
        scratch=[pltpu.VMEM((TILE, TILE), F32)] * 2,
    )
    pieces = shape(groups, columns, width)
    low_mine, high_mine = call(solve_body, (pieces, pieces), factor, side)
    y_high = exchanged(high_mine, "grp")
    high = call(high_body, shape(columns, width), y_high, high_mine, even)
    carried = lax.ppermute(high, PTS, [(i, (i + 1) % owners) for i in range(owners)])
    y_low = exchanged(low_mine, "grp")
    low, pair = call(
        low_body,
        (shape(columns, width), shape(columns, width)),
        y_low,
        low_mine,
        high_mine,
        even,
    )
    return ((low + carried).T[None], pair.T[None])


def solution(mesh):
    torus = Mesh(
        mesh.devices.reshape(8, 8, 2, mesh.shape["grp"]), ("pts_0", "pts_1", "pts_2", "grp")
    )
    placed = (P(PTS_GRP, None, None, None), P(PTS_GRP, None), P(PTS, None))
    return jax.shard_map(
        local,
        mesh=torus,
        in_specs=placed,
        out_specs=(P(PTS, None, "grp"), P(PTS, None, "grp")),
        check_vma=False,
    )
```

time: 302 us -> 161 us (0.53)
  the two profiles are of different devices: /device:TPU:32 before, /device:TPU:2 now
where the time goes in v1:
time: 161 us
  blocking collectives  86 us (53%)
  Pallas kernels  26.5 us (16%)
  starting transfers between devices  16.8 us (10%)
  between operations  14.1 us (9%)
  waiting for transfers between devices  13.9 us (9%)
  local copies, waits for them, and re-layouts  2.84 us (2%)
    all_to_all x3, blocking collectives, exchanged(): return lax.all_to_all(value, axis, 0, 0, tiled=True)  86 us
    pallas_call x9, Pallas kernels, call(): pl.pallas_call(body, out_shape=outs, scratch_shapes=scratch, compiler_par...  26.5 us
    all_to_all x3, starting transfers between devices, exchanged(): return lax.all_to_all(value, axis, 0, 0, tiled=True)  14.8 us
    all_to_all x3, waiting for transfers between devices, exchanged(): return lax.all_to_all(value, axis, 0, 0, tiled=True)  12.4 us
  transfers between devices with their start and end apart: 5, of which 3 were waited for; matrix products, arithmetic and copies ran while one was open for 0% of the time, Pallas kernels for 15%

profile of v1, /device:TPU:2, one launch (start us, length us, event | category | flops | bytes accessed | tf_op | source)
XLA Modules:
  0.0 160.8 jit_solution(14103605524086524237)
XLA Ops:
  7.2 0.0 reduce-scatter.2.cloned.1.call-start
  7.2 0.0 copy-start.2
  7.2 1.2 copy-done.2
  8.4 0.0 copy-start.3
  8.4 0.7 copy-done.3
  9.0 0.8 shard_map.50
  9.8 63.3 %all_to_all.30.rows_ref = bf16[128,2,3456]{2,1,0:T(2,128)(2,1)S(1)} all-to-all(bf16[128,2,3456]{2,1,0:T(2,128)(2,1)S(1)} %shard_map.50), channel_id=1, replica_groups=mesh['pts_0'=8,'pts_1'=8,'pts_2'=2,'grp'=4] {'pts_0','pts_1','pts_2'}, dimensions={0} | all-to-all | bytes 3538944 | tf_op jit(solution)/shard_map/all_to_all | solution.py:193
  73.1 2.4 %shard_map.56 = f32[384,1152]{1,0:T(8,128)} custom-call(bf16[128,2,3456]{2,1,0:T(2,128)(2,1)S(1)} %all_to_all.30.rows_ref), custom_call_target="tpu_custom_call" | custom-call | flops 1000000000 | bytes 1000000 | tf_op jit(solution)/shard_map/pallas_call | solution.py:26
  75.5 0.0 reduce-scatter.2.cloned.1.call-update
  75.5 0.5 shard_map.51
  76.0 11.2 %all_to_all.31.parts_ref = f32[4,192,128]{2,1,0:T(8,128)S(1)} all-to-all(f32[4,192,128]{2,1,0:T(8,128)S(1)} %bitcast.14), channel_id=1, replica_groups=mesh['pts_0'=8,'pts_1'=8,'pts_2'=2,'grp'=4] {'grp'}, dimensions={0} | all-to-all | bytes 786432 | tf_op jit(solution)/shard_map/all_to_all | solution.py:193
  87.2 0.8 shard_map.52
  87.9 4.9 %all-to-all-start.2 = ((f32[4,192,128]{2,1,0:T(8,128)}), f32[4,192,128]{2,1,0:T(8,128)S(1)}, u32[]{:S(2)}, u32[]{:S(2)}) async-start(f32[4,192,128]{2,1,0:T(8,128)} %shard_map.52), calls=%async_computation.2 | async-start | bytes 786432 | tf_op jit(solution)/shard_map/all_to_all | solution.py:193
  92.8 1.9 %shard_map.54 = f32[384,768]{1,0:T(8,128)} custom-call(bf16[128,2,3456]{2,1,0:T(2,128)(2,1)S(1)} %all_to_all.30.rows_ref), custom_call_target="tpu_custom_call" | custom-call | flops 1000000000 | bytes 1000000 | tf_op jit(solution)/shard_map/pallas_call | solution.py:26
  94.8 0.0 copy-start.4
  94.8 9.1 %all-to-all-done.2 = f32[4,192,128]{2,1,0:T(8,128)S(1)} async-done(((f32[4,192,128]{2,1,0:T(8,128)}), f32[4,192,128]{2,1,0:T(8,128)S(1)}, u32[]{:S(2)}, u32[]{:S(2)}) %all-to-all-start.2) | async-done | bytes 393248 | tf_op jit(solution)/shard_map/all_to_all | solution.py:193
  103.9 5.0 %all-to-all-start.3 = ((f32[4,96,768]{2,1,0:T(8,128)}), f32[4,96,768]{2,1,0:T(8,128)S(1)}, u32[]{:S(2)}, u32[]{:S(2)}) async-start(f32[4,96,768]{2,1,0:T(8,128)} %bitcast.4), calls=%async_computation.3 | async-start | bytes 2359296 | tf_op jit(solution)/shard_map/all_to_all | solution.py:193
  108.9 0.0 copy-done.4
  108.9 14.1 %shard_map.53.factor_ref = f32[768,128]{1,0:T(8,128)S(1)} custom-call(f32[768,128]{1,0:T(8,128)S(1)} %bitcast.13, f32[1,384]{1,0:T(1,128)S(1)} %copy-done.4), custom_call_target="tpu_custom_call" | custom-call | flops 10000000000 | bytes 1000000 | tf_op jit(solution)/shard_map/pallas_call | solution.py:26
  123.0 0.0 all-to-all-done.3.right_ref
  123.0 2.3 %shard_map.55 = (f32[4,96,384]{2,1,0:T(8,128)}, f32[4,96,384]{2,1,0:T(8,128)S(1)}) custom-call(f32[768,128]{1,0:T(8,128)S(1)} %shard_map.53.factor_ref, f32[4,96,768]{2,1,0:T(8,128)S(1)} %all-to-all-done.3.right_ref), custom_call_target="tpu_custom_call" | custom-call | tf_op jit(solution)/shard_map/pallas_call | solution.py:26
  125.3 11.6 %all_to_all.32.y_ref = f32[4,96,384]{2,1,0:T(8,128)S(1)} all-to-all(f32[4,96,384]{2,1,0:T(8,128)S(1)} %get-tuple-element.9.high_mine_ref.mine_ref), channel_id=1, replica_groups=mesh['pts_0'=8,'pts_1'=8,'pts_2'=2,'grp'=4] {'grp'}, dimensions={0} | all-to-all | bytes 1179648 | tf_op jit(solution)/shard_map/all_to_all | solution.py:193
  136.9 4.9 %all-to-all-start.4 = ((f32[4,96,384]{2,1,0:T(8,128)}), f32[4,96,384]{2,1,0:T(8,128)S(1)}, u32[]{:S(2)}, u32[]{:S(2)}) async-start(f32[4,96,384]{2,1,0:T(8,128)} %get-tuple-element.8.low_mine_ref), calls=%async_computation.4 | async-start | bytes 1179648 | tf_op jit(solution)/shard_map/all_to_all | solution.py:193
  141.8 0.0 reduce-scatter.2.cloned.1.call-done.even_ref
  141.8 0.0 copy-start
  141.8 1.0 copy-done
  142.8 0.0 copy-start.1
  142.8 0.7 shard_map.58
  143.5 1.9 %collective-permute-start = (f32[96,384]{1,0:T(8,128)S(1)}, f32[96,384]{1,0:T(8,128)S(1)}, u32[]{:S(2)}, u32[]{:S(2)}) collective-permute-start(f32[96,384]{1,0:T(8,128)S(1)} %shard_map.58), channel_id=1, source_target_pairs={{0,4},{4,8},{8,12},{12,16},{16,20},{20,24},{24,28},{28,32},{32,36}... | collective-permute-start | bytes 442376 | tf_op jit(solution)/shard_map/ppermute | solution.py:242
  145.4 3.3 %all-to-all-done.4.y_ref = f32[4,96,384]{2,1,0:T(8,128)S(1)} async-done(((f32[4,96,384]{2,1,0:T(8,128)}), f32[4,96,384]{2,1,0:T(8,128)S(1)}, u32[]{:S(2)}, u32[]{:S(2)}) %all-to-all-start.4) | async-done | bytes 589856 | tf_op jit(solution)/shard_map/all_to_all | solution.py:193
  148.7 0.0 copy-done.1
  148.7 3.0 %shard_map.57 = (f32[96,384]{1,0:T(8,128)S(1)}, f32[96,384]{1,0:T(8,128)}) custom-call(f32[4,96,384]{2,1,0:T(8,128)S(1)} %all-to-all-done.4.y_ref, f32[4,96,384]{2,1,0:T(8,128)} %get-tuple-element.8.low_mine_ref, f32[4,96,384]{2,1,0:T(8,128)S(1)} %get-tuple-element.9.high_mine_ref.mine_ref, f32[96,1152]{1,0:T(8,128)S(1)} %copy-done.1), custom_call_target="tpu_custom_call" | custom-call | tf_op jit(solution)/shard_map/pallas_call | solution.py:26
  151.8 1.5 collective-permute-done
  153.3 0.7 add_bitcast_fusion
Async XLA Ops:
  7.2 134.6 %reduce-scatter.2.cloned.1.call-start = ((), (), s32[]{:S(2)}) async-start(), calls=%async_computation.7 | async-start | bytes 2211840 | tf_op jit(solution)/shard_map/reduce_scatter | solution.py:226
  7.2 1.2 copy-start.2
  8.4 0.7 copy-start.3
  87.9 15.9 %all-to-all-start.2 = ((f32[4,192,128]{2,1,0:T(8,128)}), f32[4,192,128]{2,1,0:T(8,128)S(1)}, u32[]{:S(2)}, u32[]{:S(2)}) async-start(f32[4,192,128]{2,1,0:T(8,128)} %shard_map.52), calls=%async_computation.2 | async-start | bytes 786432 | tf_op jit(solution)/shard_map/all_to_all | solution.py:193
  94.8 14.1 %copy-start.4 = (f32[1,384]{1,0:T(1,128)S(1)}, f32[1,384]{1,0:T(1,128)}, u32[]{:S(2)}) copy-start(f32[1,384]{1,0:T(1,128)} %damping_ref.1) | copy-start | bytes 4612
  103.9 19.1 %all-to-all-start.3 = ((f32[4,96,768]{2,1,0:T(8,128)}), f32[4,96,768]{2,1,0:T(8,128)S(1)}, u32[]{:S(2)}, u32[]{:S(2)}) async-start(f32[4,96,768]{2,1,0:T(8,128)} %bitcast.4), calls=%async_computation.3 | async-start | bytes 2359296 | tf_op jit(solution)/shard_map/all_to_all | solution.py:193
  136.9 11.9 %all-to-all-start.4 = ((f32[4,96,384]{2,1,0:T(8,128)}), f32[4,96,384]{2,1,0:T(8,128)S(1)}, u32[]{:S(2)}, u32[]{:S(2)}) async-start(f32[4,96,384]{2,1,0:T(8,128)} %get-tuple-element.8.low_mine_ref), calls=%async_computation.4 | async-start | bytes 1179648 | tf_op jit(solution)/shard_map/all_to_all | solution.py:193
  141.8 1.0 copy-start
  142.8 6.0 %copy-start.1 = (f32[96,1152]{1,0:T(8,128)S(1)}, f32[96,1152]{1,0:T(8,128)}, u32[]{:S(2)}) copy-start(f32[96,1152]{1,0:T(8,128)} %reduce-scatter.2.cloned.1.call-done.even_ref) | copy-start | bytes 1327108
  143.5 9.8 %collective-permute-start = (f32[96,384]{1,0:T(8,128)S(1)}, f32[96,384]{1,0:T(8,128)S(1)}, u32[]{:S(2)}, u32[]{:S(2)}) collective-permute-start(f32[96,384]{1,0:T(8,128)S(1)} %shard_map.58), channel_id=1, source_target_pairs={{0,4},{4,8},{8,12},{12,16},{16,20},{20,24},{24,28},{28,32},{32,36}... | collective-permute-start | bytes 442376 | tf_op jit(solution)/shard_map/ppermute | solution.py:242
Sparse Core Ops, SparseCore 0:
  75.6 30.1 reduce-scatter.1

commit v2 on v1

v2 whole, which is shorter than its diff:
```python
import jax
import jax.numpy as jnp
from jax import lax
from jax.experimental import pallas as pl
from jax.experimental.pallas import tpu as pltpu
from jax.sharding import Mesh
from jax.sharding import PartitionSpec as P

PTS = ("pts_0", "pts_1", "pts_2")
PTS_GRP = ("pts_0", "pts_1", "pts_2", "grp")
F32 = jnp.float32
BF16 = jnp.bfloat16
HI = lax.Precision.HIGHEST
NN = ((1,), (0,))
NT = ((1,), (1,))
TN = ((0,), (0,))
TILE = 128
SUB = 8
PARAMS = pltpu.CompilerParams(vmem_limit_bytes=40 * 2**20)


def mm(a, b, dims, prec=None):
    return lax.dot_general(a, b, (dims, ((), ())), precision=prec, preferred_element_type=F32)


def call(body, outs, *args, cost=None, scratch=(), scalars=0):
    places = [pltpu.SMEM] * scalars + [pltpu.VMEM] * (len(args) - scalars)
    return pl.pallas_call(
        body,
        out_shape=outs,
        in_specs=[pl.BlockSpec(memory_space=place) for place in places],
        scratch_shapes=scratch,
        compiler_params=PARAMS,
        cost_estimate=cost,
    )(*args)


def cost(flops, nbytes):
    return pl.CostEstimate(flops=flops, bytes_accessed=nbytes, transcendentals=0)


def pack_body(capacity, owner_ref, rows_ref, out_ref):
    clusters, sets, points, width = rows_ref.shape
    slots = out_ref.shape[0] * capacity
    owner = owner_ref[...]
    slot = lax.broadcasted_iota(jnp.int32, (slots, points), 0)
    hit = jnp.where(owner == slot // capacity, 1.0, 0.0)
    upper = jnp.where(
        lax.broadcasted_iota(jnp.int32, (points, points), 0)
        < lax.broadcasted_iota(jnp.int32, (points, points), 1),
        1.0,
        0.0,
    )
    before = mm(hit.astype(BF16), upper.astype(BF16), NN)
    pick = jnp.where(before == (slot % capacity).astype(F32), hit, 0.0).astype(BF16)
    for k in range(clusters):
        for r in range(sets):
            at = (k * sets + r) * width
            rows = mm(pick, rows_ref[k, r], NN).astype(BF16)
            out_ref[:, :, at : at + width] = rows.reshape(-1, capacity, width)


def cluster_rows(ref, k):
    width = ref.shape[2] // 9
    at = k * 3 * width
    flat = ref[:, :, at : at + 3 * width].reshape(-1, 3 * width)
    return [flat[:, r * width : (r + 1) * width] for r in range(3)]


def summed_gram(left, right):
    return mm(left[0], right[0], TN) + mm(left[1], right[1], TN) + mm(left[2], right[2], TN)


def odd_body(rows_ref, out_ref):
    mid = cluster_rows(rows_ref, 1)
    full = summed_gram(mid, mid)
    at = 0
    for i in range(full.shape[0] // TILE):
        for j in range(i + 1):
            block = full[i * TILE : (i + 1) * TILE, j * TILE : (j + 1) * TILE]
            for k in range(out_ref.shape[0]):
                out_ref[k, at : at + TILE] = block
            at += TILE


def side_body(index_ref, rows_ref, *refs):
    piece_refs, full_ref = refs[:-1], refs[-1]
    width = full_ref.shape[0]
    columns = piece_refs[0].shape[0]
    mid = cluster_rows(rows_ref, 1)
    full_ref[:, :width] = summed_gram(cluster_rows(rows_ref, 0), mid)
    full_ref[:, width:] = summed_gram(cluster_rows(rows_ref, 2), mid)
    for k, piece_ref in enumerate(piece_refs):
        at = lax.rem(index_ref[0] + k, len(piece_refs))
        piece_ref[...] = full_ref[pl.ds(pl.multiple_of(at * columns, 8), columns), :]


def even_body(rows_ref, out_ref, last_ref):
    width = last_ref.shape[0]
    first, last = cluster_rows(rows_ref, 0), cluster_rows(rows_ref, 2)
    last_ref[...] = summed_gram(last, last)
    out_ref[:, :width] = summed_gram(first, first)
    out_ref[:, width:] = summed_gram(last, first)


def join_body(even_ref, last_ref, out_ref):
    width = last_ref.shape[0]
    out_ref[:, :width] = even_ref[:, :width] + last_ref[...]
    out_ref[:, width:] = even_ref[:, width:]


def eye(n):
    rows = lax.broadcasted_iota(jnp.int32, (n, n), 0)
    return jnp.where(rows == lax.broadcasted_iota(jnp.int32, (n, n), 1), 1.0, 0.0).astype(F32)


def factor_tile(a_ref, w_ref, panel):
    n = a_ref.shape[0]
    tiles = panel // SUB
    row = lax.broadcasted_iota(jnp.int32, (SUB, n), 0)

    def splat(value, r):
        return jnp.broadcast_to(value[r : r + 1, :], (SUB, n))

    for b in range(0, n, panel):
        pa = [a_ref[b + t * SUB : b + (t + 1) * SUB, :] for t in range(tiles)]
        pw = [w_ref[b + t * SUB : b + (t + 1) * SUB, :] for t in range(tiles)]
        for top in range(tiles):
            at = b + top * SUB
            cols = [
                {t: jnp.broadcast_to(pa[t][:, at + k : at + k + 1], (SUB, n)) for t in range(top, tiles)}
                for k in range(SUB)
            ]
            scale = jnp.ones((SUB, n), F32)
            for r in range(0, SUB, 2):
                p = splat(cols[r][top], r)
                q = splat(cols[r][top], r + 1)
                c = splat(cols[r + 1][top], r + 1)
                over = 1.0 / (p * c - q * q)
                g0, g1, g2 = c * over, q * over, p * over
                h = q * (1.0 / p)
                scale = jnp.where(row == r, p, jnp.where(row == r + 1, c - q * h, scale))
                first = top if r + 2 < SUB else top + 1
                m0, m1 = {}, {}
                for t in range(first, tiles):
                    c0, c1 = cols[r][t], cols[r + 1][t]
                    m0[t] = c0 * g0 - c1 * g1
                    m1[t] = c1 * g2 - c0 * g1
                    if t == top:
                        m0[t] = jnp.where(row > r + 1, m0[t], 0.0)
                        m1[t] = jnp.where(row > r + 1, m1[t], 0.0)
                for k in range(r + 2, SUB):
                    s0, s1 = splat(cols[k][top], r), splat(cols[k][top], r + 1)
                    for t in range(first, tiles):
                        cols[k][t] = cols[k][t] - m0[t] * s0 - m1[t] * s1
                for x in (pa, pw):
                    s0, s1 = splat(x[top], r), splat(x[top], r + 1)
                    for t in range(first, tiles):
                        x[t] = x[t] - m0[t] * s0 - m1[t] * s1
                    x[top] = jnp.where(row == r + 1, x[top] - h * s0, x[top])
            rs = lax.rsqrt(scale)
            pa[top] = pa[top] * rs
            pw[top] = pw[top] * rs
        left = jnp.concatenate(pa, axis=0)
        right = jnp.concatenate(pw, axis=0)
        w_ref[b : b + panel, :] = right
        if b + panel < n:
            u = mm(left, jnp.concatenate([left, right], axis=1), TN, HI)
            a_ref[b + panel :, :] = a_ref[b + panel :, :] - u[b + panel :, :n]
            w_ref[b + panel :, :] = w_ref[b + panel :, :] - u[b + panel :, n:]


def summed(ref, at, rows):
    value = ref[0, at : at + rows]
    for k in range(1, ref.shape[0]):
        value = value + ref[k, at : at + rows]
    return value


def factor_body(blocks_ref, damping_ref, out_ref, a_ref, w_ref):
    n = TILE
    count = damping_ref.shape[1] // n
    at, s = 0, []
    for i in range(count):
        s.append([])
        for j in range(i + 1):
            s[i].append(summed(blocks_ref, at, n))
            at += n
    for i in range(count):
        s[i][i] = s[i][i] + eye(n) * damping_ref[:, i * n : (i + 1) * n]
    for d in range(count):
        a_ref[...] = s[d][d]
        w_ref[...] = eye(n)
        factor_tile(a_ref, w_ref, 64)
        w = w_ref[...]
        out_ref[(d * (d + 1) // 2 + d) * n : (d * (d + 1) // 2 + d + 1) * n] = w
        for i in range(d + 1, count):
            s[i][d] = mm(s[i][d], w, NT, HI)
            out_ref[(i * (i + 1) // 2 + d) * n : (i * (i + 1) // 2 + d + 1) * n] = s[i][d]
        for i in range(d + 1, count):
            for k in range(d + 1, i + 1):
                s[i][k] = s[i][k] - mm(s[i][d], s[k][d], NT, HI)


def solve_body(factor_ref, *refs):
    right_refs, (low_ref, high_ref) = refs[:-2], refs[-2:]
    n = TILE
    rows, width = right_refs[0].shape[0], right_refs[0].shape[1] // 2
    count = width // n
    block = lambda i, j: factor_ref[(i * (i + 1) // 2 + j) * n : (i * (i + 1) // 2 + j + 1) * n]
    right = right_refs[0][...]
    for ref in right_refs[1:]:
        right = right + ref[...]
    right = jnp.concatenate([right[:, :width], right[:, width:]], axis=0)
    done = []
    for i in range(count):
        part = right[:, i * n : (i + 1) * n]
        for j in range(i):
            part = part - mm(done[j], block(i, j), NT, HI)
        done.append(mm(part, block(i, i), NT, HI))
        for k in range(low_ref.shape[0]):
            low_ref[k, :, i * n : (i + 1) * n] = done[i][:rows]
            high_ref[k, :, i * n : (i + 1) * n] = done[i][rows:]


def whole(ref):
    return jnp.concatenate([ref[k] for k in range(ref.shape[0])], axis=0)


def total_body(parts_ref, out_ref):
    value = parts_ref[0]
    for k in range(1, parts_ref.shape[0]):
        value = value + parts_ref[k]
    out_ref[...] = value


def high_body(y_ref, mine_ref, out_ref):
    out_ref[...] = mm(mine_ref[0], whole(y_ref), NT, HI)


def low_body(y_ref, low_mine_ref, high_mine_ref, even_ref, high_ref, diag_ref, pair_ref):
    columns, width = high_ref.shape
    mine = jnp.concatenate([low_mine_ref[0], high_mine_ref[0]], axis=0)
    u = mm(mine, whole(y_ref), NT, HI)
    diag_ref[...] = even_ref[:, :width] - u[:columns] - high_ref[...]
    pair_ref[...] = even_ref[:, width:] - u[columns:]


def exchanged(value, axis):
    return lax.all_to_all(value, axis, 0, 0, tiled=True)


def turned(value, axis, by):
    if by == 0:
        return value
    devices = lax.axis_size(axis)
    return lax.ppermute(value, axis, [(i, (i + by) % devices) for i in range(devices)])


def after(value, other):
    return lax.optimization_barrier((value, other))[0]


def shape(*dims):
    return jax.ShapeDtypeStruct(dims, F32)


def local(jacobian, owner, damping):
    points, _, _, width = jacobian.shape
    owners = lax.axis_size(PTS)
    groups = lax.axis_size("grp")
    columns = width // groups
    capacity = max(2, 2 * points // owners)
    rows = jnp.transpose(jacobian, (1, 2, 0, 3))
    segment = owner.reshape(1, points)
    tiles = (width // TILE) * (width // TILE + 1) // 2

    sent = call(
        lambda *refs: pack_body(capacity, *refs),
        jax.ShapeDtypeStruct((owners, capacity, 9 * width), BF16),
        segment,
        rows,
    )
    got = exchanged(sent, PTS)
    odd = call(odd_body, shape(groups, tiles * TILE, TILE), got, cost=cost(10**9, 10**6))
    odd = exchanged(odd, "grp")
    even, last = call(
        even_body, [shape(width, 2 * width), shape(width, width)], got, cost=cost(10**9, 10**6)
    )
    carried = turned(last, PTS, 1)
    index = lax.axis_index("grp").astype(jnp.int32).reshape(1)
    side = call(
        side_body,
        [shape(columns, 2 * width)] * groups,
        index,
        got,
        cost=cost(10**9, 10**6),
        scratch=[pltpu.VMEM((width, 2 * width), F32)],
        scalars=1,
    )
    side = [turned(piece, "grp", k) for k, piece in enumerate(side)]
    even = call(join_body, shape(width, 2 * width), even, carried)
    even = exchanged(after(even, odd).reshape(groups, columns, 2 * width), "grp")
    factor = call(
        factor_body,
        shape(tiles * TILE, TILE),
        odd,
        damping,
        cost=cost(10**10, 10**6),
        scratch=[pltpu.VMEM((TILE, TILE), F32)] * 2,
    )
    low_mine, high_mine = call(
        solve_body, [shape(groups, columns, width)] * 2, factor, *side
    )
    high_mine, even = lax.optimization_barrier((high_mine, even))
    y_high = exchanged(high_mine, "grp")
    even = call(total_body, shape(columns, 2 * width), even)
    high = call(high_body, shape(columns, width), y_high, high_mine)
    high = turned(high, PTS, 1)
    low_mine, y_high = lax.optimization_barrier((low_mine, y_high))
    y_low = exchanged(low_mine, "grp")
    diag, pair = call(
        low_body, [shape(columns, width)] * 2, y_low, low_mine, high_mine, even, high
    )
    return (diag.T[None], pair.T[None])


def solution(mesh):
    torus = Mesh(
        mesh.devices.reshape(8, 8, 2, mesh.shape["grp"]), ("pts_0", "pts_1", "pts_2", "grp")
    )
    placed = (P(PTS_GRP, None, None, None), P(PTS_GRP, None), P(PTS, None))
    return jax.shard_map(
        local,
        mesh=torus,
        in_specs=placed,
        out_specs=(P(PTS, None, "grp"), P(PTS, None, "grp")),
        check_vma=False,
    )
```

time: 161 us -> 147 us (0.913)
  between operations: 14.1 us -> 0.79 us
  starting transfers between devices: 16.8 us -> 30.1 us
  blocking collectives: 86 us -> 75 us
  waiting for transfers between devices: 13.9 us -> 9.96 us
  local copies, waits for them, and re-layouts: 2.84 us -> 4.73 us
    ppermute x1 -> x5, starting transfers between devices: 1.92 us -> 14.2 us  [turned(): lax.ppermute(value, axis, [(i, (i + by) % devices) for i in range(devices)])]
    all_to_all x3 -> x2, blocking collectives: 86 us -> 75 us  [exchanged(): return lax.all_to_all(value, axis, 0, 0, tiled=True)]
    all_to_all x3, waiting for transfers between devices: 12.4 us -> 2.16 us  [exchanged(): return lax.all_to_all(value, axis, 0, 0, tiled=True)]
    ppermute x1 -> x5, waiting for transfers between devices: 1.52 us -> 7.8 us  [turned(): lax.ppermute(value, axis, [(i, (i + by) % devices) for i in range(devices)])]
    unnamed x10 -> x16, local copies, waits for them, and re-layouts: 2.84 us -> 4.73 us
    pallas_call x9 -> x10, Pallas kernels: 26.5 us -> 25.9 us  [call(): pl.pallas_call(body, out_shape=outs, in_specs=[pl.BlockSpec(memory_space=...]
  transfers between devices with their start and end apart: 5 -> 8, of which waited for: 3 -> 2; matrix products, arithmetic and copies ran while one was open for 0% -> 0% of each run, Pallas kernels for 15% -> 15%
where the time goes in v2:
time: 147 us; the launch traced here: 146 us
  blocking collectives  75 us (51%)
  starting transfers between devices  30.1 us (20%)
  Pallas kernels  25.9 us (18%)
  waiting for transfers between devices  9.96 us (7%)
  local copies, waits for them, and re-layouts  4.73 us (3%)
    all_to_all x2, blocking collectives, exchanged(): return lax.all_to_all(value, axis, 0, 0, tiled=True)  75 us
    pallas_call x10, Pallas kernels, call(): pl.pallas_call(body, out_shape=outs, in_specs=[pl.BlockSpec(memory_space=...  25.9 us
    all_to_all x3, starting transfers between devices, exchanged(): return lax.all_to_all(value, axis, 0, 0, tiled=True)  15.8 us
    ppermute x5, starting transfers between devices, turned(): lax.ppermute(value, axis, [(i, (i + by) % devices) for i in range(devices)])  14.2 us
    ppermute x5, waiting for transfers between devices, turned(): lax.ppermute(value, axis, [(i, (i + by) % devices) for i in range(devices)])  7.8 us
    unnamed x16, local copies, waits for them, and re-layouts  4.73 us
  transfers between devices with their start and end apart: 8, of which 2 were waited for; matrix products, arithmetic and copies ran while one was open for 0% of the time, Pallas kernels for 15%

profile of v2, /device:TPU:2, one launch (start us, length us, event | category | flops | bytes accessed | tf_op | source)
XLA Modules:
  0.0 146.5 jit_solution(9359933385442460593)
XLA Ops:
  0.6 0.0 copy-start.3
  0.6 1.2 copy-done.3
  1.8 0.0 copy-start.6
  1.8 0.7 copy-done.6
  2.5 0.8 shard_map.50
  3.2 63.3 %all_to_all.25.rows_ref = bf16[128,2,3456]{2,1,0:T(2,128)(2,1)S(1)} all-to-all(bf16[128,2,3456]{2,1,0:T(2,128)(2,1)S(1)} %shard_map.50), channel_id=1, replica_groups=mesh['pts_0'=8,'pts_1'=8,'pts_2'=2,'grp'=4] {'pts_0','pts_1','pts_2'}, dimensions={0} | all-to-all | bytes 3538944 | tf_op jit(solution)/shard_map/all_to_all | solution.py:250
  66.5 0.6 shard_map.51
  67.1 0.0 copy-start
  67.1 1.2 copy-done
  68.2 4.8 %all-to-all-start.1 = ((f32[4,768,128]{2,1,0:T(8,128)}), f32[4,768,128]{2,1,0:T(8,128)S(1)}, u32[]{:S(2)}, u32[]{:S(2)}) async-start(f32[4,768,128]{2,1,0:T(8,128)} %copy-done), calls=%async_computation.1 | async-start | bytes 3145728 | tf_op jit(solution)/shard_map/all_to_all | solution.py:250
  73.0 1.4 shard_map.55
  74.4 0.0 copy-start.1
  74.4 1.0 copy-done.1
  75.4 1.9 %collective-permute-start.3 = (f32[384,384]{1,0:T(8,128)}, f32[384,384]{1,0:T(8,128)}, u32[]{:S(2)}, u32[]{:S(2)}) collective-permute-start(f32[384,384]{1,0:T(8,128)} %get-tuple-element.23), channel_id=1, source_target_pairs={{0,4},{4,8},{8,12},{12,16},{16,20},{20,24},{24,28},{28,32},{32,36}... | collective-permute-start | bytes 1769480 | tf_op jit(solution)/shard_map/ppermute | solution.py:257
  77.3 0.0 copy-start.2
  77.4 1.9 %shard_map.53 = (f32[96,768]{1,0:T(8,128)S(1)}, f32[96,768]{1,0:T(8,128)}, f32[96,768]{1,0:T(8,128)}, f32[96,768]{1,0:T(8,128)}) custom-call(s32[1]{0:T(128)} %bitcast.2.index_ref, bf16[128,2,3456]{2,1,0:T(2,128)(2,1)S(1)} %all_to_all.25.rows_ref), custom_call_target="tpu_custom_call" | custom-call | flops 1000000000 | bytes 1000000 | tf_op jit(solution)/shard_map/pallas_call | solution.py:28
  79.3 0.0 copy-start.4
  79.3 0.7 copy-done.4
  80.0 3.4 %collective-permute-start = (f32[96,768]{1,0:T(8,128)}, f32[96,768]{1,0:T(8,128)S(1)}, u32[]{:S(2)}, u32[]{:S(2)}) collective-permute-start(f32[96,768]{1,0:T(8,128)} %get-tuple-element.17), channel_id=1, source_target_pairs={{0,1},{1,2},{2,3},{3,0},{4,5},{5,6},{6,7},{7,4},{8,9},{9,10},{10,1... | collective-permute-start | bytes 884744 | tf_op jit(solution)/shard_map/ppermute | solution.py:257
  83.4 2.5 %collective-permute-start.1 = (f32[96,768]{1,0:T(8,128)}, f32[96,768]{1,0:T(8,128)S(1)}, u32[]{:S(2)}, u32[]{:S(2)}) collective-permute-start(f32[96,768]{1,0:T(8,128)} %get-tuple-element.18), channel_id=1, source_target_pairs={{0,2},{1,3},{2,0},{3,1},{4,6},{5,7},{6,4},{7,5},{8,10},{9,11},{10,... | collective-permute-start | bytes 884744 | tf_op jit(solution)/shard_map/ppermute | solution.py:257
  85.9 4.5 %collective-permute-start.2 = (f32[96,768]{1,0:T(8,128)}, f32[96,768]{1,0:T(8,128)}, u32[]{:S(2)}, u32[]{:S(2)}) collective-permute-start(f32[96,768]{1,0:T(8,128)} %get-tuple-element.19), channel_id=1, source_target_pairs={{0,3},{1,0},{2,1},{3,2},{4,7},{5,4},{6,5},{7,6},{8,11},{9,8},{10,9... | collective-permute-start | bytes 884744 | tf_op jit(solution)/shard_map/ppermute | solution.py:257
  90.5 0.0 collective-permute-done.3.last_ref
  90.5 0.0 copy-done.2
  90.5 2.2 %shard_map.56 = f32[384,768]{1,0:T(8,128)} custom-call(f32[384,768]{1,0:T(8,128)S(1)} %copy-done.2, f32[384,384]{1,0:T(8,128)} %collective-permute-done.3.last_ref), custom_call_target="tpu_custom_call" | custom-call | tf_op jit(solution)/shard_map/pallas_call | solution.py:28
  92.7 0.0 copy-start.7
  92.7 0.0 all-to-all-done.1.blocks_ref
  92.7 6.1 %all-to-all-start.2 = ((f32[4,96,768]{2,1,0:T(8,128)}), f32[4,96,768]{2,1,0:T(8,128)S(1)}, u32[]{:S(2)}, u32[]{:S(2)}) async-start(f32[4,96,768]{2,1,0:T(8,128)} %bitcast.3), calls=%async_computation.2 | async-start | bytes 2359296 | tf_op jit(solution)/shard_map/all_to_all | solution.py:250
  98.8 0.0 copy-done.7
  98.8 0.0 copy-start.5
  98.8 12.5 %shard_map.52.factor_ref = f32[768,128]{1,0:T(8,128)S(1)} custom-call(f32[4,768,128]{2,1,0:T(8,128)S(1)} %all-to-all-done.1.blocks_ref, f32[1,384]{1,0:T(1,128)S(1)} %copy-done.7), custom_call_target="tpu_custom_call" | custom-call | flops 10000000000 | bytes 1000000 | tf_op jit(solution)/shard_map/pallas_call | solution.py:28
  111.3 0.0 collective-permute-done.refs_1_
  111.3 0.0 collective-permute-done.1.refs_2_
  111.3 0.0 collective-permute-done.2.refs_3_
  111.3 0.0 copy-done.5
  111.3 3.3 %shard_map.54 = (f32[4,96,384]{2,1,0:T(8,128)}, f32[4,96,384]{2,1,0:T(8,128)S(1)}) custom-call(f32[768,128]{1,0:T(8,128)S(1)} %shard_map.52.factor_ref, f32[96,768]{1,0:T(8,128)S(1)} %copy-done.5, f32[96,768]{1,0:T(8,128)S(1)} %collective-permute-done.refs_1_, f32[96,768]{1,0:T(8,128)S(1)} %collective-permute-done.1.refs_2_, ...), custom_call_target="tpu_custom_call" | custom-call | tf_op jit(solution)/shard_map/pallas_call | solution.py:28
  114.6 2.2 %all-to-all-done.2.parts_ref = f32[4,96,768]{2,1,0:T(8,128)S(1)} async-done(((f32[4,96,768]{2,1,0:T(8,128)}), f32[4,96,768]{2,1,0:T(8,128)S(1)}, u32[]{:S(2)}, u32[]{:S(2)}) %all-to-all-start.2) | async-done | bytes 1179680 | tf_op jit(solution)/shard_map/all_to_all | solution.py:250
  116.8 11.7 %all_to_all.26.y_ref = f32[4,96,384]{2,1,0:T(8,128)S(1)} all-to-all(f32[4,96,384]{2,1,0:T(8,128)S(1)} %get-tuple-element.25.mine_ref.high_mine_ref), channel_id=1, replica_groups=mesh['pts_0'=8,'pts_1'=8,'pts_2'=2,'grp'=4] {'grp'}, dimensions={0} | all-to-all | bytes 1179648 | tf_op jit(solution)/shard_map/all_to_all | solution.py:250
  128.5 4.9 %all-to-all-start.4 = ((f32[4,96,384]{2,1,0:T(8,128)}), f32[4,96,384]{2,1,0:T(8,128)S(1)}, u32[]{:S(2)}, u32[]{:S(2)}) async-start(f32[4,96,384]{2,1,0:T(8,128)} %get-tuple-element.26.low_mine_ref), calls=%async_computation.4 | async-start | bytes 1179648 | tf_op jit(solution)/shard_map/all_to_all | solution.py:250
  133.4 0.7 shard_map.58
  134.1 1.9 %collective-permute-start.4 = (f32[96,384]{1,0:T(8,128)S(1)}, f32[96,384]{1,0:T(8,128)S(1)}, u32[]{:S(2)}, u32[]{:S(2)}) collective-permute-start(f32[96,384]{1,0:T(8,128)S(1)} %shard_map.58), channel_id=1, source_target_pairs={{0,4},{4,8},{8,12},{12,16},{16,20},{20,24},{24,28},{28,32},{32,36}... | collective-permute-start | bytes 442376 | tf_op jit(solution)/shard_map/ppermute | solution.py:257
  136.0 0.1 shard_map.57.even_ref
  136.1 7.8 %collective-permute-done.4.high_ref = f32[96,384]{1,0:T(8,128)S(1)} collective-permute-done((f32[96,384]{1,0:T(8,128)S(1)}, f32[96,384]{1,0:T(8,128)S(1)}, u32[]{:S(2)}, u32[]{:S(2)}) %collective-permute-start.4) | collective-permute-done | bytes 147488 | tf_op jit(solution)/shard_map/ppermute | solution.py:257
  143.9 0.0 all-to-all-done.4.y_ref
  143.9 2.6 %shard_map.59 = (f32[96,384]{1,0:T(8,128)}, f32[96,384]{1,0:T(8,128)}) custom-call(f32[4,96,384]{2,1,0:T(8,128)S(1)} %all-to-all-done.4.y_ref, f32[4,96,384]{2,1,0:T(8,128)} %get-tuple-element.26.low_mine_ref, f32[4,96,384]{2,1,0:T(8,128)S(1)} %get-tuple-element.25.mine_ref.high_mine_ref, f32[96,768]{1,0:T(8,128)S(1)} %shard_map.57.even_ref, ...), custom_call_target="tpu_custom_call" | custom-call | tf_op jit(solution)/shard_map/pallas_call | solution.py:28
Async XLA Ops:
  0.6 1.2 copy-start.3
  1.8 0.7 copy-start.6
  67.1 1.2 copy-start
  68.2 24.5 %all-to-all-start.1 = ((f32[4,768,128]{2,1,0:T(8,128)}), f32[4,768,128]{2,1,0:T(8,128)S(1)}, u32[]{:S(2)}, u32[]{:S(2)}) async-start(f32[4,768,128]{2,1,0:T(8,128)} %copy-done), calls=%async_computation.1 | async-start | bytes 3145728 | tf_op jit(solution)/shard_map/all_to_all | solution.py:250
  74.4 1.0 copy-start.1
  75.4 15.0 %collective-permute-start.3 = (f32[384,384]{1,0:T(8,128)}, f32[384,384]{1,0:T(8,128)}, u32[]{:S(2)}, u32[]{:S(2)}) collective-permute-start(f32[384,384]{1,0:T(8,128)} %get-tuple-element.23), channel_id=1, source_target_pairs={{0,4},{4,8},{8,12},{12,16},{16,20},{20,24},{24,28},{28,32},{32,36}... | collective-permute-start | bytes 1769480 | tf_op jit(solution)/shard_map/ppermute | solution.py:257
  77.3 13.1 %copy-start.2 = (f32[384,768]{1,0:T(8,128)S(1)}, f32[384,768]{1,0:T(8,128)}, u32[]{:S(2)}) copy-start(f32[384,768]{1,0:T(8,128)} %copy-done.1) | copy-start | bytes 3538948
  79.3 0.7 copy-start.4
  80.0 31.3 %collective-permute-start = (f32[96,768]{1,0:T(8,128)}, f32[96,768]{1,0:T(8,128)S(1)}, u32[]{:S(2)}, u32[]{:S(2)}) collective-permute-start(f32[96,768]{1,0:T(8,128)} %get-tuple-element.17), channel_id=1, source_target_pairs={{0,1},{1,2},{2,3},{3,0},{4,5},{5,6},{6,7},{7,4},{8,9},{9,10},{10,1... | collective-permute-start | bytes 884744 | tf_op jit(solution)/shard_map/ppermute | solution.py:257
  83.4 27.9 %collective-permute-start.1 = (f32[96,768]{1,0:T(8,128)}, f32[96,768]{1,0:T(8,128)S(1)}, u32[]{:S(2)}, u32[]{:S(2)}) collective-permute-start(f32[96,768]{1,0:T(8,128)} %get-tuple-element.18), channel_id=1, source_target_pairs={{0,2},{1,3},{2,0},{3,1},{4,6},{5,7},{6,4},{7,5},{8,10},{9,11},{10,... | collective-permute-start | bytes 884744 | tf_op jit(solution)/shard_map/ppermute | solution.py:257
  85.9 25.4 %collective-permute-start.2 = (f32[96,768]{1,0:T(8,128)}, f32[96,768]{1,0:T(8,128)}, u32[]{:S(2)}, u32[]{:S(2)}) collective-permute-start(f32[96,768]{1,0:T(8,128)} %get-tuple-element.19), channel_id=1, source_target_pairs={{0,3},{1,0},{2,1},{3,2},{4,7},{5,4},{6,5},{7,6},{8,11},{9,8},{10,9... | collective-permute-start | bytes 884744 | tf_op jit(solution)/shard_map/ppermute | solution.py:257
  92.7 6.1 %copy-start.7 = (f32[1,384]{1,0:T(1,128)S(1)}, f32[1,384]{1,0:T(1,128)}, u32[]{:S(2)}) copy-start(f32[1,384]{1,0:T(1,128)} %damping_ref.1) | copy-start | bytes 4612
  92.7 24.1 %all-to-all-start.2 = ((f32[4,96,768]{2,1,0:T(8,128)}), f32[4,96,768]{2,1,0:T(8,128)S(1)}, u32[]{:S(2)}, u32[]{:S(2)}) async-start(f32[4,96,768]{2,1,0:T(8,128)} %bitcast.3), calls=%async_computation.2 | async-start | bytes 2359296 | tf_op jit(solution)/shard_map/all_to_all | solution.py:250
  98.8 12.5 %copy-start.5 = (f32[96,768]{1,0:T(8,128)S(1)}, f32[96,768]{1,0:T(8,128)}, u32[]{:S(2)}) copy-start(f32[96,768]{1,0:T(8,128)} %copy-done.4) | copy-start | bytes 884740
  128.5 15.4 %all-to-all-start.4 = ((f32[4,96,384]{2,1,0:T(8,128)}), f32[4,96,384]{2,1,0:T(8,128)S(1)}, u32[]{:S(2)}, u32[]{:S(2)}) async-start(f32[4,96,384]{2,1,0:T(8,128)} %get-tuple-element.26.low_mine_ref), calls=%async_computation.4 | async-start | bytes 1179648 | tf_op jit(solution)/shard_map/all_to_all | solution.py:250
  134.1 9.8 %collective-permute-start.4 = (f32[96,384]{1,0:T(8,128)S(1)}, f32[96,384]{1,0:T(8,128)S(1)}, u32[]{:S(2)}, u32[]{:S(2)}) collective-permute-start(f32[96,384]{1,0:T(8,128)S(1)} %shard_map.58), channel_id=1, source_target_pairs={{0,4},{4,8},{8,12},{12,16},{16,20},{20,24},{24,28},{28,32},{32,36}... | collective-permute-start | bytes 442376 | tf_op jit(solution)/shard_map/ppermute | solution.py:257

commit v3 on v2

--- a/solution.py
+++ b/solution.py
@@ -71,16 +71,31 @@
     return mm(left[0], right[0], TN) + mm(left[1], right[1], TN) + mm(left[2], right[2], TN)
 
 
-def odd_body(rows_ref, out_ref):
+def odd_body(rows_ref, out_ref, packed_ref, sems):
     mid = cluster_rows(rows_ref, 1)
     full = summed_gram(mid, mid)
-    at = 0
-    for i in range(full.shape[0] // TILE):
+    count = full.shape[0] // TILE
+    block = lambda i, j: full[i * TILE : (i + 1) * TILE, j * TILE : (j + 1) * TILE]
+    lower = lax.broadcasted_iota(jnp.int32, (TILE, TILE), 0) >= lax.broadcasted_iota(
+        jnp.int32, (TILE, TILE), 1
+    )
+    packed_ref[:TILE] = jnp.where(lower, block(0, 0), block(1, 1))
+    at = TILE
+    for i in range(1, count):
         for j in range(i + 1):
-            block = full[i * TILE : (i + 1) * TILE, j * TILE : (j + 1) * TILE]
-            for k in range(out_ref.shape[0]):
-                out_ref[k, at : at + TILE] = block
-            at += TILE
+            if (i, j) != (1, 1):
+                packed_ref[at : at + TILE] = block(i, j)
+                at += TILE
+    diagonal = jnp.sum(block(1, 1) * eye(TILE), axis=0, keepdims=True)
+    packed_ref[at:] = jnp.broadcast_to(diagonal, (SUB, TILE))
+    copies = [
+        pltpu.make_async_copy(packed_ref, out_ref.at[k], sems.at[k])
+        for k in range(out_ref.shape[0])
+    ]
+    for copy in copies:
+        copy.start()
+    for copy in copies:
+        copy.wait()
 
 
 def side_body(index_ref, rows_ref, *refs):
@@ -95,18 +110,16 @@
         piece_ref[...] = full_ref[pl.ds(pl.multiple_of(at * columns, 8), columns), :]
 
 
-def even_body(rows_ref, out_ref, last_ref):
-    width = last_ref.shape[0]
+def last_body(rows_ref, out_ref):
+    last = cluster_rows(rows_ref, 2)
+    out_ref[...] = summed_gram(last, last)
+
+
+def even_body(rows_ref, carried_ref, out_ref):
+    width = carried_ref.shape[0]
     first, last = cluster_rows(rows_ref, 0), cluster_rows(rows_ref, 2)
-    last_ref[...] = summed_gram(last, last)
-    out_ref[:, :width] = summed_gram(first, first)
+    out_ref[:, :width] = summed_gram(first, first) + carried_ref[...]
     out_ref[:, width:] = summed_gram(last, first)
-
-
-def join_body(even_ref, last_ref, out_ref):
-    width = last_ref.shape[0]
-    out_ref[:, :width] = even_ref[:, :width] + last_ref[...]
-    out_ref[:, width:] = even_ref[:, width:]
 
 
 def eye(n):
@@ -180,15 +193,24 @@
 def factor_body(blocks_ref, damping_ref, out_ref, a_ref, w_ref):
     n = TILE
     count = damping_ref.shape[1] // n
-    at, s = 0, []
-    for i in range(count):
+    packed = summed(blocks_ref, 0, n)
+    turned_over = packed.T
+    row = lax.broadcasted_iota(jnp.int32, (n, n), 0)
+    col = lax.broadcasted_iota(jnp.int32, (n, n), 1)
+    at, s = n, [[jnp.where(row >= col, packed, turned_over)]]
+    for i in range(1, count):
         s.append([])
         for j in range(i + 1):
-            s[i].append(summed(blocks_ref, at, n))
-            at += n
+            if (i, j) != (1, 1):
+                s[i].append(summed(blocks_ref, at, n))
+                at += n
+            else:
+                s[i].append(jnp.where(row < col, packed, turned_over))
+    diagonal = summed(blocks_ref, at, SUB)[:1]
+    s[1][1] = jnp.where(row == col, diagonal, s[1][1])
     for i in range(count):
         s[i][i] = s[i][i] + eye(n) * damping_ref[:, i * n : (i + 1) * n]
-    for d in range(count):
+    for d in range(count - 1):
         a_ref[...] = s[d][d]
         w_ref[...] = eye(n)
         factor_tile(a_ref, w_ref, 64)
@@ -200,14 +222,17 @@
         for i in range(d + 1, count):
             for k in range(d + 1, i + 1):
                 s[i][k] = s[i][k] - mm(s[i][d], s[k][d], NT, HI)
+    out_ref[-n:] = s[-1][-1]
 
 
 def solve_body(factor_ref, *refs):
-    right_refs, (low_ref, high_ref) = refs[:-2], refs[-2:]
+    right_refs, (low_ref, high_ref, a_ref, w_ref) = refs[:-4], refs[-4:]
     n = TILE
     rows, width = right_refs[0].shape[0], right_refs[0].shape[1] // 2
     count = width // n
     block = lambda i, j: factor_ref[(i * (i + 1) // 2 + j) * n : (i * (i + 1) // 2 + j + 1) * n]
+    a_ref[...] = block(count - 1, count - 1)
+    w_ref[...] = eye(n)
     right = right_refs[0][...]
     for ref in right_refs[1:]:
         right = right + ref[...]
@@ -217,10 +242,15 @@
         part = right[:, i * n : (i + 1) * n]
         for j in range(i):
             part = part - mm(done[j], block(i, j), NT, HI)
-        done.append(mm(part, block(i, i), NT, HI))
+        if i == count - 1:
+            factor_tile(a_ref, w_ref, 64)
+            inverse = w_ref[...]
+        else:
+            inverse = block(i, i)
+        done.append(mm(part, inverse, NT, HI))
         for k in range(low_ref.shape[0]):
             low_ref[k, :, i * n : (i + 1) * n] = done[i][:rows]
-            high_ref[k, :, i * n : (i + 1) * n] = done[i][rows:]
+        high_ref[:, i * n : (i + 1) * n] = done[i][rows:]
 
 
 def whole(ref):
@@ -235,12 +265,12 @@
 
 
 def high_body(y_ref, mine_ref, out_ref):
-    out_ref[...] = mm(mine_ref[0], whole(y_ref), NT, HI)
+    out_ref[...] = mm(mine_ref[...], whole(y_ref), NT, HI)
 
 
 def low_body(y_ref, low_mine_ref, high_mine_ref, even_ref, high_ref, diag_ref, pair_ref):
     columns, width = high_ref.shape
-    mine = jnp.concatenate([low_mine_ref[0], high_mine_ref[0]], axis=0)
+    mine = jnp.concatenate([low_mine_ref[0], high_mine_ref[...]], axis=0)
     u = mm(mine, whole(y_ref), NT, HI)
     diag_ref[...] = even_ref[:, :width] - u[:columns] - high_ref[...]
     pair_ref[...] = even_ref[:, width:] - u[columns:]
@@ -282,11 +312,18 @@
         rows,
     )
     got = exchanged(sent, PTS)
-    odd = call(odd_body, shape(groups, tiles * TILE, TILE), got, cost=cost(10**9, 10**6))
+    packed = (tiles - 1) * TILE + SUB
+    odd = pl.pallas_call(
+        odd_body,
+        out_shape=shape(groups, packed, TILE),
+        in_specs=[pl.BlockSpec(memory_space=pltpu.VMEM)],
+        out_specs=pl.BlockSpec(memory_space=pltpu.HBM),
+        scratch_shapes=[pltpu.VMEM((packed, TILE), F32), pltpu.SemaphoreType.DMA((groups,))],
+        compiler_params=PARAMS,
+        cost_estimate=cost(10**9, 10**6),
+    )(got)
     odd = exchanged(odd, "grp")
-    even, last = call(
-        even_body, [shape(width, 2 * width), shape(width, width)], got, cost=cost(10**9, 10**6)
-    )
+    last = call(last_body, shape(width, width), got, cost=cost(10**9, 10**6))
     carried = turned(last, PTS, 1)
     index = lax.axis_index("grp").astype(jnp.int32).reshape(1)
     side = call(
@@ -299,7 +336,7 @@
         scalars=1,
     )
     side = [turned(piece, "grp", k) for k, piece in enumerate(side)]
-    even = call(join_body, shape(width, 2 * width), even, carried)
+    even = call(even_body, shape(width, 2 * width), got, carried, cost=cost(10**9, 10**6))
     even = exchanged(after(even, odd).reshape(groups, columns, 2 * width), "grp")
     factor = call(
         factor_body,
@@ -310,15 +347,19 @@
         scratch=[pltpu.VMEM((TILE, TILE), F32)] * 2,
     )
     low_mine, high_mine = call(
-        solve_body, [shape(groups, columns, width)] * 2, factor, *side
-    )
-    high_mine, even = lax.optimization_barrier((high_mine, even))
-    y_high = exchanged(high_mine, "grp")
+        solve_body,
+        [shape(groups, columns, width), shape(columns, width)],
+        factor,
+        *side,
+        cost=cost(3 * 10**9, 10**6),
+        scratch=[pltpu.VMEM((TILE, TILE), F32)] * 2,
+    )
+    y_high = lax.all_gather(high_mine, "grp", axis=0, tiled=False)
+    low_mine, y_high, even = lax.optimization_barrier((low_mine, y_high, even))
+    y_low = exchanged(low_mine, "grp")
     even = call(total_body, shape(columns, 2 * width), even)
     high = call(high_body, shape(columns, width), y_high, high_mine)
     high = turned(high, PTS, 1)
-    low_mine, y_high = lax.optimization_barrier((low_mine, y_high))
-    y_low = exchanged(low_mine, "grp")
     diag, pair = call(
         low_body, [shape(columns, width)] * 2, y_low, low_mine, high_mine, even, high
     )

time: 147 us -> 145 us (0.986)
  waiting for transfers between devices: 9.96 us -> 7.81 us
  blocking collectives: 75 us -> 76.9 us
    all_gather x0 -> x1, blocking collectives: none -> 13.6 us  [local(): y_high = lax.all_gather(high_mine, 'grp', axis=0, tiled=False)]
    all_to_all x2 -> x1, blocking collectives: 75 us -> 63.3 us  [exchanged(): return lax.all_to_all(value, axis, 0, 0, tiled=True)]
    all_to_all x3, waiting for transfers between devices: 2.16 us -> 0.01 us  [exchanged(): return lax.all_to_all(value, axis, 0, 0, tiled=True)]
    pallas_call x10 -> x9, Pallas kernels: 25.9 us -> 24.2 us  [call(): pl.pallas_call(body, out_shape=outs, in_specs=[pl.BlockSpec(memory_space=...]
    unnamed x16 -> x14, local copies, waits for them, and re-layouts: 4.73 us -> 4.62 us
  transfers between devices with their start and end apart: 8 -> 8, of which waited for: 2 -> 1; matrix products, arithmetic and copies ran while one was open for 0% -> 0% of each run, Pallas kernels for 15% -> 14%
where the time goes in v3:
time: 145 us; the launch traced here: 144 us
  blocking collectives  76.9 us (53%)
  starting transfers between devices  28.7 us (20%)
  Pallas kernels  25.2 us (17%)
  waiting for transfers between devices  7.81 us (5%)
  local copies, waits for them, and re-layouts  4.62 us (3%)
    all_to_all x1, blocking collectives, exchanged(): return lax.all_to_all(value, axis, 0, 0, tiled=True)  63.3 us
    pallas_call x9, Pallas kernels, call(): pl.pallas_call(body, out_shape=outs, in_specs=[pl.BlockSpec(memory_space=...  24.2 us
    all_to_all x3, starting transfers between devices, exchanged(): return lax.all_to_all(value, axis, 0, 0, tiled=True)  14.4 us
    ppermute x5, starting transfers between devices, turned(): lax.ppermute(value, axis, [(i, (i + by) % devices) for i in range(devices)])  14.2 us
    all_gather x1, blocking collectives, local(): y_high = lax.all_gather(high_mine, 'grp', axis=0, tiled=False)  13.6 us
    ppermute x5, waiting for transfers between devices, turned(): lax.ppermute(value, axis, [(i, (i + by) % devices) for i in range(devices)])  7.8 us
    unnamed x14, local copies, waits for them, and re-layouts  4.62 us
  transfers between devices with their start and end apart: 8, of which 1 were waited for; matrix products, arithmetic and copies ran while one was open for 0% of the time, Pallas kernels for 14%

profile of v3, /device:TPU:2, one launch (start us, length us, event | category | flops | bytes accessed | tf_op | source)
XLA Modules:
  0.0 143.9 jit_solution(12487500813600408409)
XLA Ops:
  0.6 0.0 copy-start.2
  0.6 1.2 copy-done.2
  1.8 0.0 copy-start.3
  1.8 0.7 copy-done.3
  2.5 0.8 shard_map.50
  3.2 63.3 %all_to_all.20.rows_ref = bf16[128,2,3456]{2,1,0:T(2,128)(2,1)S(1)} all-to-all(bf16[128,2,3456]{2,1,0:T(2,128)(2,1)S(1)} %shard_map.50), channel_id=1, replica_groups=mesh['pts_0'=8,'pts_1'=8,'pts_2'=2,'grp'=4] {'pts_0','pts_1','pts_2'}, dimensions={0} | all-to-all | bytes 3538944 | tf_op jit(solution)/shard_map/all_to_all | solution.py:280
  66.5 1.0 shard_map.51
  67.5 0.0 copy-start
  67.5 1.1 copy-done
  68.6 4.8 %all-to-all-start.1 = ((f32[4,648,128]{2,1,0:T(8,128)}), f32[4,648,128]{2,1,0:T(8,128)S(1)}, u32[]{:S(2)}, u32[]{:S(2)}) async-start(f32[4,648,128]{2,1,0:T(8,128)} %copy-done), calls=%async_computation.1 | async-start | bytes 2654208 | tf_op jit(solution)/shard_map/all_to_all | solution.py:280
  73.4 1.3 shard_map.55
  74.8 1.9 %collective-permute-start.3 = (f32[384,384]{1,0:T(8,128)}, f32[384,384]{1,0:T(8,128)}, u32[]{:S(2)}, u32[]{:S(2)}) collective-permute-start(f32[384,384]{1,0:T(8,128)} %shard_map.55), channel_id=1, source_target_pairs={{0,4},{4,8},{8,12},{12,16},{16,20},{20,24},{24,28},{28,32},{32,36}... | collective-permute-start | bytes 1769480 | tf_op jit(solution)/shard_map/ppermute | solution.py:287
  76.7 2.0 %shard_map.53 = (f32[96,768]{1,0:T(8,128)S(1)}, f32[96,768]{1,0:T(8,128)}, f32[96,768]{1,0:T(8,128)}, f32[96,768]{1,0:T(8,128)}) custom-call(s32[1]{0:T(128)} %bitcast.2.index_ref, bf16[128,2,3456]{2,1,0:T(2,128)(2,1)S(1)} %all_to_all.20.rows_ref), custom_call_target="tpu_custom_call" | custom-call | flops 1000000000 | bytes 1000000 | tf_op jit(solution)/shard_map/pallas_call | solution.py:28
  78.7 0.0 copy-start.5
  78.7 0.7 copy-done.5
  79.4 3.3 %collective-permute-start = (f32[96,768]{1,0:T(8,128)}, f32[96,768]{1,0:T(8,128)S(1)}, u32[]{:S(2)}, u32[]{:S(2)}) collective-permute-start(f32[96,768]{1,0:T(8,128)} %get-tuple-element.15), channel_id=1, source_target_pairs={{0,1},{1,2},{2,3},{3,0},{4,5},{5,6},{6,7},{7,4},{8,9},{9,10},{10,1... | collective-permute-start | bytes 884744 | tf_op jit(solution)/shard_map/ppermute | solution.py:287
  82.7 2.6 %collective-permute-start.1 = (f32[96,768]{1,0:T(8,128)}, f32[96,768]{1,0:T(8,128)}, u32[]{:S(2)}, u32[]{:S(2)}) collective-permute-start(f32[96,768]{1,0:T(8,128)} %get-tuple-element.16), channel_id=1, source_target_pairs={{0,2},{1,3},{2,0},{3,1},{4,6},{5,7},{6,4},{7,5},{8,10},{9,11},{10,... | collective-permute-start | bytes 884744 | tf_op jit(solution)/shard_map/ppermute | solution.py:287
  85.3 4.5 %collective-permute-start.2 = (f32[96,768]{1,0:T(8,128)}, f32[96,768]{1,0:T(8,128)}, u32[]{:S(2)}, u32[]{:S(2)}) collective-permute-start(f32[96,768]{1,0:T(8,128)} %get-tuple-element.17), channel_id=1, source_target_pairs={{0,3},{1,0},{2,1},{3,2},{4,7},{5,4},{6,5},{7,6},{8,11},{9,8},{10,9... | collective-permute-start | bytes 884744 | tf_op jit(solution)/shard_map/ppermute | solution.py:287
  89.8 0.0 collective-permute-done.3.carried_ref
  89.8 1.9 %shard_map.56 = f32[384,768]{1,0:T(8,128)S(1)} custom-call(bf16[128,2,3456]{2,1,0:T(2,128)(2,1)S(1)} %all_to_all.20.rows_ref, f32[384,384]{1,0:T(8,128)} %collective-permute-done.3.carried_ref), custom_call_target="tpu_custom_call" | custom-call | flops 1000000000 | bytes 1000000 | tf_op jit(solution)/shard_map/pallas_call | solution.py:28
  91.7 0.0 copy-start.1
  91.7 1.0 copy-done.1
  92.7 0.0 copy-start.4
  92.7 0.0 all-to-all-done.1.blocks_ref
  92.8 5.1 %all-to-all-start.2 = ((f32[4,96,768]{2,1,0:T(8,128)}), f32[4,96,768]{2,1,0:T(8,128)S(1)}, u32[]{:S(2)}, u32[]{:S(2)}) async-start(f32[4,96,768]{2,1,0:T(8,128)} %bitcast.12), calls=%async_computation.2 | async-start | bytes 2359296 | tf_op jit(solution)/shard_map/all_to_all | solution.py:280
  97.8 0.0 copy-done.4
  97.8 0.0 copy-start.6
  97.8 8.8 %shard_map.52.factor_ref = f32[768,128]{1,0:T(8,128)S(1)} custom-call(f32[4,648,128]{2,1,0:T(8,128)S(1)} %all-to-all-done.1.blocks_ref, f32[1,384]{1,0:T(1,128)S(1)} %copy-done.4), custom_call_target="tpu_custom_call" | custom-call | flops 10000000000 | bytes 1000000 | tf_op jit(solution)/shard_map/pallas_call | solution.py:28
  106.7 0.0 collective-permute-done.refs_1_
  106.7 0.0 collective-permute-done.1.refs_2_
  106.7 0.0 collective-permute-done.2.refs_3_
  106.7 0.0 copy-done.6
  106.7 6.0 %shard_map.54 = (f32[4,96,384]{2,1,0:T(8,128)}, f32[96,384]{1,0:T(8,128)S(1)}) custom-call(f32[768,128]{1,0:T(8,128)S(1)} %shard_map.52.factor_ref, f32[96,768]{1,0:T(8,128)S(1)} %copy-done.6, f32[96,768]{1,0:T(8,128)S(1)} %collective-permute-done.refs_1_, f32[96,768]{1,0:T(8,128)} %collective-permute-done.1.refs_2_, f32[96,768]{1,0:T(8,128)} %collective-permute-done.2.refs_3_), custom_call_target="tpu_custom_call" | custom-call | flops 3000000000 | bytes 1000000 | tf_op jit(solution)/shard_map/pallas_call | solution.py:28
  112.7 13.6 %all-gather = f32[384,384]{1,0:T(8,128)S(1)} all-gather(f32[96,384]{1,0:T(8,128)S(1)} %get-tuple-element.19.mine_ref.high_mine_ref), channel_id=2, replica_groups=mesh['pts_0'=8,'pts_1'=8,'pts_2'=2,'grp'=4] {'grp'}, dimensions={0}, use_global_device_ids=true | all-gather | bytes 737280 | tf_op jit(solution)/shard_map/all_gather | solution.py:357
  126.3 0.0 all-to-all-done.2.parts_ref
  126.3 4.5 %all-to-all-start.3 = ((f32[4,96,384]{2,1,0:T(8,128)}), f32[4,96,384]{2,1,0:T(8,128)S(1)}, u32[]{:S(2)}, u32[]{:S(2)}) async-start(f32[4,96,384]{2,1,0:T(8,128)} %get-tuple-element.21.low_mine_ref), calls=%async_computation.3 | async-start | bytes 1179648 | tf_op jit(solution)/shard_map/all_to_all | solution.py:280
  130.8 0.7 shard_map.58
  131.5 1.9 %collective-permute-start.4 = (f32[96,384]{1,0:T(8,128)S(1)}, f32[96,384]{1,0:T(8,128)S(1)}, u32[]{:S(2)}, u32[]{:S(2)}) collective-permute-start(f32[96,384]{1,0:T(8,128)S(1)} %shard_map.58), channel_id=1, source_target_pairs={{0,4},{4,8},{8,12},{12,16},{16,20},{20,24},{24,28},{28,32},{32,36}... | collective-permute-start | bytes 442376 | tf_op jit(solution)/shard_map/ppermute | solution.py:287
  133.4 0.1 shard_map.57.even_ref
  133.5 7.8 %collective-permute-done.4.high_ref = f32[96,384]{1,0:T(8,128)S(1)} collective-permute-done((f32[96,384]{1,0:T(8,128)S(1)}, f32[96,384]{1,0:T(8,128)S(1)}, u32[]{:S(2)}, u32[]{:S(2)}) %collective-permute-start.4) | collective-permute-done | bytes 147488 | tf_op jit(solution)/shard_map/ppermute | solution.py:287
  141.3 0.0 all-to-all-done.3.y_ref
  141.3 2.6 %shard_map.59 = (f32[96,384]{1,0:T(8,128)}, f32[96,384]{1,0:T(8,128)}) custom-call(f32[4,96,384]{2,1,0:T(8,128)S(1)} %all-to-all-done.3.y_ref, f32[4,96,384]{2,1,0:T(8,128)} %get-tuple-element.21.low_mine_ref, f32[96,384]{1,0:T(8,128)S(1)} %get-tuple-element.19.mine_ref.high_mine_ref, f32[96,768]{1,0:T(8,128)S(1)} %shard_map.57.even_ref, ...), custom_call_target="tpu_custom_call" | custom-call | tf_op jit(solution)/shard_map/pallas_call | solution.py:28
Async XLA Ops:
  0.6 1.2 copy-start.2
  1.8 0.7 copy-start.3
  67.5 1.1 copy-start
  68.6 24.2 %all-to-all-start.1 = ((f32[4,648,128]{2,1,0:T(8,128)}), f32[4,648,128]{2,1,0:T(8,128)S(1)}, u32[]{:S(2)}, u32[]{:S(2)}) async-start(f32[4,648,128]{2,1,0:T(8,128)} %copy-done), calls=%async_computation.1 | async-start | bytes 2654208 | tf_op jit(solution)/shard_map/all_to_all | solution.py:280
  74.8 15.1 %collective-permute-start.3 = (f32[384,384]{1,0:T(8,128)}, f32[384,384]{1,0:T(8,128)}, u32[]{:S(2)}, u32[]{:S(2)}) collective-permute-start(f32[384,384]{1,0:T(8,128)} %shard_map.55), channel_id=1, source_target_pairs={{0,4},{4,8},{8,12},{12,16},{16,20},{20,24},{24,28},{28,32},{32,36}... | collective-permute-start | bytes 1769480 | tf_op jit(solution)/shard_map/ppermute | solution.py:287
  78.7 0.7 copy-start.5
  79.4 27.3 %collective-permute-start = (f32[96,768]{1,0:T(8,128)}, f32[96,768]{1,0:T(8,128)S(1)}, u32[]{:S(2)}, u32[]{:S(2)}) collective-permute-start(f32[96,768]{1,0:T(8,128)} %get-tuple-element.15), channel_id=1, source_target_pairs={{0,1},{1,2},{2,3},{3,0},{4,5},{5,6},{6,7},{7,4},{8,9},{9,10},{10,1... | collective-permute-start | bytes 884744 | tf_op jit(solution)/shard_map/ppermute | solution.py:287
  82.7 24.0 %collective-permute-start.1 = (f32[96,768]{1,0:T(8,128)}, f32[96,768]{1,0:T(8,128)}, u32[]{:S(2)}, u32[]{:S(2)}) collective-permute-start(f32[96,768]{1,0:T(8,128)} %get-tuple-element.16), channel_id=1, source_target_pairs={{0,2},{1,3},{2,0},{3,1},{4,6},{5,7},{6,4},{7,5},{8,10},{9,11},{10,... | collective-permute-start | bytes 884744 | tf_op jit(solution)/shard_map/ppermute | solution.py:287
  85.3 21.4 %collective-permute-start.2 = (f32[96,768]{1,0:T(8,128)}, f32[96,768]{1,0:T(8,128)}, u32[]{:S(2)}, u32[]{:S(2)}) collective-permute-start(f32[96,768]{1,0:T(8,128)} %get-tuple-element.17), channel_id=1, source_target_pairs={{0,3},{1,0},{2,1},{3,2},{4,7},{5,4},{6,5},{7,6},{8,11},{9,8},{10,9... | collective-permute-start | bytes 884744 | tf_op jit(solution)/shard_map/ppermute | solution.py:287
  91.7 1.0 copy-start.1
  92.7 5.1 %copy-start.4 = (f32[1,384]{1,0:T(1,128)S(1)}, f32[1,384]{1,0:T(1,128)}, u32[]{:S(2)}) copy-start(f32[1,384]{1,0:T(1,128)} %damping_ref.1) | copy-start | bytes 4612
  92.8 33.6 %all-to-all-start.2 = ((f32[4,96,768]{2,1,0:T(8,128)}), f32[4,96,768]{2,1,0:T(8,128)S(1)}, u32[]{:S(2)}, u32[]{:S(2)}) async-start(f32[4,96,768]{2,1,0:T(8,128)} %bitcast.12), calls=%async_computation.2 | async-start | bytes 2359296 | tf_op jit(solution)/shard_map/all_to_all | solution.py:280
  97.8 8.9 %copy-start.6 = (f32[96,768]{1,0:T(8,128)S(1)}, f32[96,768]{1,0:T(8,128)}, u32[]{:S(2)}) copy-start(f32[96,768]{1,0:T(8,128)} %copy-done.5) | copy-start | bytes 884740
  126.3 15.0 %all-to-all-start.3 = ((f32[4,96,384]{2,1,0:T(8,128)}), f32[4,96,384]{2,1,0:T(8,128)S(1)}, u32[]{:S(2)}, u32[]{:S(2)}) async-start(f32[4,96,384]{2,1,0:T(8,128)} %get-tuple-element.21.low_mine_ref), calls=%async_computation.3 | async-start | bytes 1179648 | tf_op jit(solution)/shard_map/all_to_all | solution.py:280
  131.5 9.8 %collective-permute-start.4 = (f32[96,384]{1,0:T(8,128)S(1)}, f32[96,384]{1,0:T(8,128)S(1)}, u32[]{:S(2)}, u32[]{:S(2)}) collective-permute-start(f32[96,384]{1,0:T(8,128)S(1)} %shard_map.58), channel_id=1, source_target_pairs={{0,4},{4,8},{8,12},{12,16},{16,20},{20,24},{24,28},{28,32},{32,36}... | collective-permute-start | bytes 442376 | tf_op jit(solution)/shard_map/ppermute | solution.py:287

commit v4 on v3

--- a/solution.py
+++ b/solution.py
@@ -268,11 +268,11 @@
     out_ref[...] = mm(mine_ref[...], whole(y_ref), NT, HI)
 
 
-def low_body(y_ref, low_mine_ref, high_mine_ref, even_ref, high_ref, diag_ref, pair_ref):
-    columns, width = high_ref.shape
+def low_body(y_ref, low_mine_ref, high_mine_ref, even_ref, diag_ref, pair_ref):
+    columns, width = diag_ref.shape
     mine = jnp.concatenate([low_mine_ref[0], high_mine_ref[...]], axis=0)
     u = mm(mine, whole(y_ref), NT, HI)
-    diag_ref[...] = even_ref[:, :width] - u[:columns] - high_ref[...]
+    diag_ref[...] = even_ref[:, :width] - u[:columns]
     pair_ref[...] = even_ref[:, width:] - u[columns:]
 
 
@@ -355,15 +355,15 @@
         scratch=[pltpu.VMEM((TILE, TILE), F32)] * 2,
     )
     y_high = lax.all_gather(high_mine, "grp", axis=0, tiled=False)
-    low_mine, y_high, even = lax.optimization_barrier((low_mine, y_high, even))
+    high = call(high_body, shape(columns, width), y_high, high_mine)
+    low_mine, high, even = lax.optimization_barrier((low_mine, high, even))
+    high = turned(high, PTS, 1)
     y_low = exchanged(low_mine, "grp")
     even = call(total_body, shape(columns, 2 * width), even)
-    high = call(high_body, shape(columns, width), y_high, high_mine)
-    high = turned(high, PTS, 1)
     diag, pair = call(
-        low_body, [shape(columns, width)] * 2, y_low, low_mine, high_mine, even, high
-    )
-    return (diag.T[None], pair.T[None])
+        low_body, [shape(columns, width)] * 2, y_low, low_mine, high_mine, even
+    )
+    return ((diag - high).T[None], pair.T[None])
 
 
 def solution(mesh):

time: 145 us -> 143 us (0.986)
  the two profiles are of different devices: /device:TPU:2 before, /device:TPU:8 now
where the time goes in v4:
time: 143 us; the launch traced here: 142 us
  blocking collectives  76.7 us (54%)
  starting transfers between devices  27.9 us (20%)
  Pallas kernels  25.1 us (18%)
  waiting for transfers between devices  6.47 us (5%)
  local copies, waits for them, and re-layouts  4.62 us (3%)
    all_to_all x1, blocking collectives, exchanged(): return lax.all_to_all(value, axis, 0, 0, tiled=True)  62.9 us
    pallas_call x9, Pallas kernels, call(): pl.pallas_call(body, out_shape=outs, in_specs=[pl.BlockSpec(memory_space=...  24.1 us
    ppermute x5, starting transfers between devices, turned(): lax.ppermute(value, axis, [(i, (i + by) % devices) for i in range(devices)])  15.7 us
    all_gather x1, blocking collectives, local(): y_high = lax.all_gather(high_mine, 'grp', axis=0, tiled=False)  13.8 us
    all_to_all x3, starting transfers between devices, exchanged(): return lax.all_to_all(value, axis, 0, 0, tiled=True)  12.3 us
    all_to_all x3, waiting for transfers between devices, exchanged(): return lax.all_to_all(value, axis, 0, 0, tiled=True)  6.46 us
    unnamed x14, local copies, waits for them, and re-layouts  4.62 us
  transfers between devices with their start and end apart: 8, of which 1 were waited for; matrix products, arithmetic and copies ran while one was open for 0% of the time, Pallas kernels for 16%

profile of v4, /device:TPU:8, one launch (start us, length us, event | category | flops | bytes accessed | tf_op | source)
XLA Modules:
  0.0 142.4 jit_solution(11947344430693857754)
XLA Ops:
  0.6 0.0 copy-start.2
  0.6 1.2 copy-done.2
  1.8 0.0 copy-start.3
  1.8 0.7 copy-done.3
  2.5 0.8 shard_map.50
  3.2 62.9 %all_to_all.20.rows_ref = bf16[128,2,3456]{2,1,0:T(2,128)(2,1)S(1)} all-to-all(bf16[128,2,3456]{2,1,0:T(2,128)(2,1)S(1)} %shard_map.50), channel_id=1, replica_groups=mesh['pts_0'=8,'pts_1'=8,'pts_2'=2,'grp'=4] {'pts_0','pts_1','pts_2'}, dimensions={0} | all-to-all | bytes 3538944 | tf_op jit(solution)/shard_map/all_to_all | solution.py:280
  66.2 1.0 shard_map.51
  67.2 0.0 copy-start
  67.2 1.1 copy-done
  68.3 4.3 %all-to-all-start.1 = ((f32[4,648,128]{2,1,0:T(8,128)}), f32[4,648,128]{2,1,0:T(8,128)S(1)}, u32[]{:S(2)}, u32[]{:S(2)}) async-start(f32[4,648,128]{2,1,0:T(8,128)} %copy-done), calls=%async_computation.1 | async-start | bytes 2654208 | tf_op jit(solution)/shard_map/all_to_all | solution.py:280
  72.6 1.3 shard_map.56
  73.9 1.9 %collective-permute-start.3 = (f32[384,384]{1,0:T(8,128)}, f32[384,384]{1,0:T(8,128)}, u32[]{:S(2)}, u32[]{:S(2)}) collective-permute-start(f32[384,384]{1,0:T(8,128)} %shard_map.56), channel_id=1, source_target_pairs={{0,4},{4,8},{8,12},{12,16},{16,20},{20,24},{24,28},{28,32},{32,36}... | collective-permute-start | bytes 1769480 | tf_op jit(solution)/shard_map/ppermute | solution.py:287
  75.8 2.0 %shard_map.53 = (f32[96,768]{1,0:T(8,128)S(1)}, f32[96,768]{1,0:T(8,128)}, f32[96,768]{1,0:T(8,128)}, f32[96,768]{1,0:T(8,128)}) custom-call(s32[1]{0:T(128)} %bitcast.2.index_ref, bf16[128,2,3456]{2,1,0:T(2,128)(2,1)S(1)} %all_to_all.20.rows_ref), custom_call_target="tpu_custom_call" | custom-call | flops 1000000000 | bytes 1000000 | tf_op jit(solution)/shard_map/pallas_call | solution.py:28
  77.8 0.0 copy-start.5
  77.8 0.7 copy-done.5
  78.5 3.9 %collective-permute-start = (f32[96,768]{1,0:T(8,128)}, f32[96,768]{1,0:T(8,128)S(1)}, u32[]{:S(2)}, u32[]{:S(2)}) collective-permute-start(f32[96,768]{1,0:T(8,128)} %get-tuple-element.15), channel_id=1, source_target_pairs={{0,1},{1,2},{2,3},{3,0},{4,5},{5,6},{6,7},{7,4},{8,9},{9,10},{10,1... | collective-permute-start | bytes 884744 | tf_op jit(solution)/shard_map/ppermute | solution.py:287
  82.4 4.6 %collective-permute-start.1 = (f32[96,768]{1,0:T(8,128)}, f32[96,768]{1,0:T(8,128)}, u32[]{:S(2)}, u32[]{:S(2)}) collective-permute-start(f32[96,768]{1,0:T(8,128)} %get-tuple-element.16), channel_id=1, source_target_pairs={{0,2},{1,3},{2,0},{3,1},{4,6},{5,7},{6,4},{7,5},{8,10},{9,11},{10,... | collective-permute-start | bytes 884744 | tf_op jit(solution)/shard_map/ppermute | solution.py:287
  87.0 3.4 %collective-permute-start.2 = (f32[96,768]{1,0:T(8,128)}, f32[96,768]{1,0:T(8,128)}, u32[]{:S(2)}, u32[]{:S(2)}) collective-permute-start(f32[96,768]{1,0:T(8,128)} %get-tuple-element.17), channel_id=1, source_target_pairs={{0,3},{1,0},{2,1},{3,2},{4,7},{5,4},{6,5},{7,6},{8,11},{9,8},{10,9... | collective-permute-start | bytes 884744 | tf_op jit(solution)/shard_map/ppermute | solution.py:287
  90.4 0.0 collective-permute-done.3.carried_ref
  90.4 1.9 %shard_map.57 = f32[384,768]{1,0:T(8,128)S(1)} custom-call(bf16[128,2,3456]{2,1,0:T(2,128)(2,1)S(1)} %all_to_all.20.rows_ref, f32[384,384]{1,0:T(8,128)} %collective-permute-done.3.carried_ref), custom_call_target="tpu_custom_call" | custom-call | flops 1000000000 | bytes 1000000 | tf_op jit(solution)/shard_map/pallas_call | solution.py:28
  92.3 0.0 copy-start.1
  92.3 1.0 copy-done.1
  93.4 0.0 copy-start.4
  93.4 0.0 all-to-all-done.1.blocks_ref
  93.4 3.8 %all-to-all-start.2 = ((f32[4,96,768]{2,1,0:T(8,128)}), f32[4,96,768]{2,1,0:T(8,128)S(1)}, u32[]{:S(2)}, u32[]{:S(2)}) async-start(f32[4,96,768]{2,1,0:T(8,128)} %bitcast.13), calls=%async_computation.2 | async-start | bytes 2359296 | tf_op jit(solution)/shard_map/all_to_all | solution.py:280
  97.2 0.0 copy-done.4
  97.2 0.0 copy-start.6
  97.2 8.8 %shard_map.52.factor_ref = f32[768,128]{1,0:T(8,128)S(1)} custom-call(f32[4,648,128]{2,1,0:T(8,128)S(1)} %all-to-all-done.1.blocks_ref, f32[1,384]{1,0:T(1,128)S(1)} %copy-done.4), custom_call_target="tpu_custom_call" | custom-call | flops 10000000000 | bytes 1000000 | tf_op jit(solution)/shard_map/pallas_call | solution.py:28
  106.1 0.0 collective-permute-done.refs_1_
  106.1 0.0 collective-permute-done.1.refs_2_
  106.1 0.0 collective-permute-done.2.refs_3_
  106.1 0.0 copy-done.6
  106.1 6.0 %shard_map.54 = (f32[4,96,384]{2,1,0:T(8,128)}, f32[96,384]{1,0:T(8,128)S(1)}) custom-call(f32[768,128]{1,0:T(8,128)S(1)} %shard_map.52.factor_ref, f32[96,768]{1,0:T(8,128)S(1)} %copy-done.6, f32[96,768]{1,0:T(8,128)S(1)} %collective-permute-done.refs_1_, f32[96,768]{1,0:T(8,128)} %collective-permute-done.1.refs_2_, f32[96,768]{1,0:T(8,128)} %collective-permute-done.2.refs_3_), custom_call_target="tpu_custom_call" | custom-call | flops 3000000000 | bytes 1000000 | tf_op jit(solution)/shard_map/pallas_call | solution.py:28
  112.1 13.8 %all-gather = f32[384,384]{1,0:T(8,128)S(1)} all-gather(f32[96,384]{1,0:T(8,128)S(1)} %get-tuple-element.19.mine_ref.high_mine_ref), channel_id=2, replica_groups=mesh['pts_0'=8,'pts_1'=8,'pts_2'=2,'grp'=4] {'grp'}, dimensions={0}, use_global_device_ids=true | all-gather | bytes 737280 | tf_op jit(solution)/shard_map/all_gather | solution.py:357
  125.9 0.7 shard_map.55
  126.6 0.0 all-to-all-done.2.parts_ref
  126.6 4.1 %all-to-all-start.3 = ((f32[4,96,384]{2,1,0:T(8,128)}), f32[4,96,384]{2,1,0:T(8,128)S(1)}, u32[]{:S(2)}, u32[]{:S(2)}) async-start(f32[4,96,384]{2,1,0:T(8,128)} %get-tuple-element.21.low_mine_ref), calls=%async_computation.3 | async-start | bytes 1179648 | tf_op jit(solution)/shard_map/all_to_all | solution.py:280
  130.7 1.9 %collective-permute-start.4 = (f32[96,384]{1,0:T(8,128)S(1)}, f32[96,384]{1,0:T(8,128)S(1)}, u32[]{:S(2)}, u32[]{:S(2)}) collective-permute-start(f32[96,384]{1,0:T(8,128)S(1)} %shard_map.55), channel_id=1, source_target_pairs={{0,4},{4,8},{8,12},{12,16},{16,20},{20,24},{24,28},{28,32},{32,36}... | collective-permute-start | bytes 442376 | tf_op jit(solution)/shard_map/ppermute | solution.py:287
  132.6 0.1 shard_map.58.even_ref
  132.7 6.5 %all-to-all-done.3.y_ref = f32[4,96,384]{2,1,0:T(8,128)S(1)} async-done(((f32[4,96,384]{2,1,0:T(8,128)}), f32[4,96,384]{2,1,0:T(8,128)S(1)}, u32[]{:S(2)}, u32[]{:S(2)}) %all-to-all-start.3) | async-done | bytes 589856 | tf_op jit(solution)/shard_map/all_to_all | solution.py:280
  139.2 2.5 %shard_map.59 = (f32[96,384]{1,0:T(8,128)S(1)}, f32[96,384]{1,0:T(8,128)}) custom-call(f32[4,96,384]{2,1,0:T(8,128)S(1)} %all-to-all-done.3.y_ref, f32[4,96,384]{2,1,0:T(8,128)} %get-tuple-element.21.low_mine_ref, f32[96,384]{1,0:T(8,128)S(1)} %get-tuple-element.19.mine_ref.high_mine_ref, f32[96,768]{1,0:T(8,128)S(1)} %shard_map.58.even_ref), custom_call_target="tpu_custom_call" | custom-call | tf_op jit(solution)/shard_map/pallas_call | solution.py:28
  141.7 0.0 collective-permute-done.4
  141.7 0.7 subtract_bitcast_fusion
Async XLA Ops:
  0.6 1.2 copy-start.2
  1.8 0.7 copy-start.3
  67.2 1.1 copy-start
  68.3 25.1 %all-to-all-start.1 = ((f32[4,648,128]{2,1,0:T(8,128)}), f32[4,648,128]{2,1,0:T(8,128)S(1)}, u32[]{:S(2)}, u32[]{:S(2)}) async-start(f32[4,648,128]{2,1,0:T(8,128)} %copy-done), calls=%async_computation.1 | async-start | bytes 2654208 | tf_op jit(solution)/shard_map/all_to_all | solution.py:280
  73.9 16.5 %collective-permute-start.3 = (f32[384,384]{1,0:T(8,128)}, f32[384,384]{1,0:T(8,128)}, u32[]{:S(2)}, u32[]{:S(2)}) collective-permute-start(f32[384,384]{1,0:T(8,128)} %shard_map.56), channel_id=1, source_target_pairs={{0,4},{4,8},{8,12},{12,16},{16,20},{20,24},{24,28},{28,32},{32,36}... | collective-permute-start | bytes 1769480 | tf_op jit(solution)/shard_map/ppermute | solution.py:287
  77.8 0.7 copy-start.5
  78.5 27.6 %collective-permute-start = (f32[96,768]{1,0:T(8,128)}, f32[96,768]{1,0:T(8,128)S(1)}, u32[]{:S(2)}, u32[]{:S(2)}) collective-permute-start(f32[96,768]{1,0:T(8,128)} %get-tuple-element.15), channel_id=1, source_target_pairs={{0,1},{1,2},{2,3},{3,0},{4,5},{5,6},{6,7},{7,4},{8,9},{9,10},{10,1... | collective-permute-start | bytes 884744 | tf_op jit(solution)/shard_map/ppermute | solution.py:287
  82.4 23.6 %collective-permute-start.1 = (f32[96,768]{1,0:T(8,128)}, f32[96,768]{1,0:T(8,128)}, u32[]{:S(2)}, u32[]{:S(2)}) collective-permute-start(f32[96,768]{1,0:T(8,128)} %get-tuple-element.16), channel_id=1, source_target_pairs={{0,2},{1,3},{2,0},{3,1},{4,6},{5,7},{6,4},{7,5},{8,10},{9,11},{10,... | collective-permute-start | bytes 884744 | tf_op jit(solution)/shard_map/ppermute | solution.py:287
  87.0 19.1 %collective-permute-start.2 = (f32[96,768]{1,0:T(8,128)}, f32[96,768]{1,0:T(8,128)}, u32[]{:S(2)}, u32[]{:S(2)}) collective-permute-start(f32[96,768]{1,0:T(8,128)} %get-tuple-element.17), channel_id=1, source_target_pairs={{0,3},{1,0},{2,1},{3,2},{4,7},{5,4},{6,5},{7,6},{8,11},{9,8},{10,9... | collective-permute-start | bytes 884744 | tf_op jit(solution)/shard_map/ppermute | solution.py:287
  92.3 1.0 copy-start.1
  93.4 3.9 %copy-start.4 = (f32[1,384]{1,0:T(1,128)S(1)}, f32[1,384]{1,0:T(1,128)}, u32[]{:S(2)}) copy-start(f32[1,384]{1,0:T(1,128)} %damping_ref.1) | copy-start | bytes 4612
  93.4 33.2 %all-to-all-start.2 = ((f32[4,96,768]{2,1,0:T(8,128)}), f32[4,96,768]{2,1,0:T(8,128)S(1)}, u32[]{:S(2)}, u32[]{:S(2)}) async-start(f32[4,96,768]{2,1,0:T(8,128)} %bitcast.13), calls=%async_computation.2 | async-start | bytes 2359296 | tf_op jit(solution)/shard_map/all_to_all | solution.py:280
  97.2 8.9 %copy-start.6 = (f32[96,768]{1,0:T(8,128)S(1)}, f32[96,768]{1,0:T(8,128)}, u32[]{:S(2)}) copy-start(f32[96,768]{1,0:T(8,128)} %copy-done.5) | copy-start | bytes 884740
  126.6 12.6 %all-to-all-start.3 = ((f32[4,96,384]{2,1,0:T(8,128)}), f32[4,96,384]{2,1,0:T(8,128)S(1)}, u32[]{:S(2)}, u32[]{:S(2)}) async-start(f32[4,96,384]{2,1,0:T(8,128)} %get-tuple-element.21.low_mine_ref), calls=%async_computation.3 | async-start | bytes 1179648 | tf_op jit(solution)/shard_map/all_to_all | solution.py:280
  130.7 11.0 %collective-permute-start.4 = (f32[96,384]{1,0:T(8,128)S(1)}, f32[96,384]{1,0:T(8,128)S(1)}, u32[]{:S(2)}, u32[]{:S(2)}) collective-permute-start(f32[96,384]{1,0:T(8,128)S(1)} %shard_map.55), channel_id=1, source_target_pairs={{0,4},{4,8},{8,12},{12,16},{16,20},{20,24},{24,28},{28,32},{32,36}... | collective-permute-start | bytes 442376 | tf_op jit(solution)/shard_map/ppermute | solution.py:287
